TPU v7x, 512 devices: a whole 4x8x8 slice. The times are simulated.
512 devices in a mesh: feat: 8 (over z), vert: 64 (over y, x, core).
Axes of the slice: x: 4, y: 8, z: 8, core: 2. Of those that a mesh axis runs over, the one named last changes fastest.
Arguments:
- features: bfloat16 [49152, 1024], P('vert', 'feat'), may hold values from -6 to 6
- adjacency: bfloat16 [49152, 2304], P('vert'), may hold values from 0 to 2, as said below
- w_self: bfloat16 [1024, 256], P('feat'), may hold values from -0.1875 to 0.1875
- w_neigh: bfloat16 [1024, 256], P('feat'), may hold values from -0.375 to 0.375
- bias: float32 [256], replicated, may hold values from -3 to 3
- cotangent: bfloat16 [49152, 256], P('vert'), may hold values from -6 to 6
Outputs:
- hidden: bfloat16 [49152, 256], P('vert', 'feat')
- grad_features: bfloat16 [49152, 1024], P('vert', 'feat')
- grad_self: float32 [1024, 256], P('feat')
- grad_neigh: float32 [1024, 256], P('feat')
Inputs may be any that keep to these rules, and one draw needn't show every extreme that they name: `adjacency`: entries are 0 or positive edge weights; a few per row are positive.
All inputs are finite; a program needn't handle non-finite values.
Results may differ from a plain program's by a relative error of at most 0.0053.
Values may be sent and summed in bfloat16 or wider, within the bound.
No kernel may reach another device: no remote copies, remote signals or barrier semaphores. Data moves between devices by JAX's collectives and lax.ppermute only.
A program may use at most 64 MiB of HBM per device.

v0:
```python
import jax
import jax.numpy as jnp
from jax import lax
from jax.sharding import PartitionSpec as P


def extended(array, sides, width):
    for axis, dim in sides:
        size, length = (lax.axis_size(axis), array.shape[dim])
        up = [(i, (i + 1) % size) for i in range(size - 1)]
        down = [(j, i) for i, j in up]
        last = lax.slice_in_dim(array, length - width, length, axis=dim)
        leading = lax.slice_in_dim(array, 0, width, axis=dim)
        before = lax.ppermute(last, axis, up)
        after = lax.ppermute(leading, axis, down)
        array = jnp.concatenate([before, array, after], axis=dim)
    return array


def shifted(block, axis, distance):
    devices = range(lax.axis_size(axis))
    route = [(i - distance, i) for i in devices if i - distance in devices]
    return lax.ppermute(block, axis, route)


def body(features, adjacency, w_self, w_neigh, bias, cotangent):
    rows = features.shape[0]
    window = extended(features, (("vert", 0),), rows)
    deg = 1.0 + jnp.sum(adjacency.astype(jnp.float32), axis=1)
    agg = (jnp.dot(adjacency, window, preferred_element_type=jnp.float32) / deg[:, None]).astype(
        jnp.bfloat16
    )
    partial_value = jnp.dot(features, w_self, preferred_element_type=jnp.float32) + jnp.dot(
        agg, w_neigh, preferred_element_type=jnp.float32
    )
    shards = lax.axis_size("feat")
    width = bias.shape[0] // shards
    offset = lax.axis_index("feat") * width
    share = lax.psum_scatter(partial_value, "feat", scatter_dimension=1, tiled=True)
    pre = share + lax.dynamic_slice_in_dim(bias, offset, width)
    sig = jax.nn.sigmoid(pre)
    hidden = (pre * sig).astype(jnp.bfloat16)
    upstream = lax.dynamic_slice_in_dim(cotangent, offset, width, 1).astype(jnp.float32)
    dpre_part = (upstream * sig * (1.0 + pre * (1.0 - sig))).astype(jnp.bfloat16)
    dpre = lax.all_gather(dpre_part, "feat", axis=1, tiled=True)
    contract = (((1,), (1,)), ((), ()))
    scaled = (
        lax.dot_general(dpre, w_neigh, contract, preferred_element_type=jnp.float32) / deg[:, None]
    ).astype(jnp.bfloat16)
    back = lax.dot_general(
        adjacency, scaled, (((0,), (0,)), ((), ())), preferred_element_type=jnp.float32
    )
    from_next = shifted(back[:rows].astype(jnp.bfloat16), "vert", -1).astype(jnp.float32)
    from_prev = shifted(back[2 * rows :], "vert", 1)
    grad_self_part = lax.dot_general(
        features, dpre, (((0,), (0,)), ((), ())), preferred_element_type=jnp.float32
    )
    grad_neigh_part = lax.dot_general(
        agg, dpre, (((0,), (0,)), ((), ())), preferred_element_type=jnp.float32
    )
    grad_self, grad_neigh = lax.psum((grad_self_part, grad_neigh_part), "vert")
    own_term = lax.dot_general(dpre, w_self, contract, preferred_element_type=jnp.float32)
    grad_features = (own_term + back[rows : 2 * rows] + from_next + from_prev).astype(jnp.bfloat16)
    return (hidden, grad_features, grad_self, grad_neigh)


def solution(mesh):
    placed = (
        P("vert", "feat"),
        P("vert", None),
        P("feat", None),
        P("feat", None),
        P(),
        P("vert", None),
    )
    return jax.shard_map(
        body,
        mesh=mesh,
        in_specs=placed,
        out_specs=(P("vert", "feat"), P("vert", "feat"), P("feat", None), P("feat", None)),
        check_vma=False,
    )
```

profile of v0, /device:TPU:1, one launch (start us, length us, event | category | flops | bytes accessed | tf_op | source)
XLA Modules:
  0.0 303.8 jit_solution(919865270012496078)
XLA Ops:
  7.2 0.0 copy-start
  7.2 0.0 copy-start.2
  7.2 0.0 reduce-scatter.2.cloned.1.call-start
  7.2 0.0 copy-start.1
  7.2 9.0 %collective-permute-start.1 = (bf16[768,128]{1,0:T(8,128)(2,1)}, bf16[768,128]{1,0:T(8,128)(2,1)S(1)}, u32[]{:S(2)}, u32[]{:S(2)}) collective-permute-start(bf16[768,128]{1,0:T(8,128)(2,1)} %param.6), channel_id=1, source_target_pairs={{1,0},{2,1},{3,2},{4,3},{5,4},{6,5},{7,6},{8,7},{9,8},{10,9},{11,1... | collective-permute-start | bytes 589832 | tf_op jit(solution)/shard_map/ppermute | solution.py:15
  16.3 1.9 collective-permute-start
  18.2 1.2 fusion.9
  19.5 2.5 convert_reduce_fusion
  22.0 0.0 copy-start.3
  22.0 0.0 copy-start.5
  22.0 0.0 collective-permute-done.1
  22.1 0.0 collective-permute-done
  22.1 0.0 copy-done.2
  22.1 0.0 copy-done.1
  22.1 1.3 fusion.1
  23.4 0.0 copy-done.3
  23.4 1.2 convolution_add_fusion
  24.6 0.0 reduce-scatter.2.cloned.1.call-update
  24.6 0.0 all-reduce.3.cloned.1.call-start
  24.7 0.0 copy-done
  24.7 0.1 constant_dynamic-slice_fusion
  24.8 0.1 copy.14
  24.9 0.0 copy-done.5
  24.9 0.1 dynamic_slice.6
  25.0 39.1 %reduce-scatter.2.cloned.1.call-done = f32[768,32]{0,1:T(8,128)} async-done(((f32[768,256]{0,1:T(8,128)}), f32[768,32]{0,1:T(8,128)}) %reduce-scatter.2.cloned.1.call-update) | async-done | bytes 98320 | tf_op jit(solution)/shard_map/reduce_scatter | solution.py:39
  64.1 1.6 multiply_convert_fusion
  65.8 18.6 %all_gather.3 = bf16[768,256]{0,1:T(8,128)(2,1)S(1)} all-gather(bf16[768,32]{0,1:T(8,128)(2,1)S(1)} %get-tuple-element.10), channel_id=1, replica_groups=mesh['feat'=8,'vert'=64] {'feat'}, dimensions={1}, use_global_device_ids=true | all-gather | bytes 442368 | tf_op jit(solution)/shard_map/all_gather | solution.py:45
  84.4 0.0 copy-start.4
  84.4 3.8 %convolution_bitcast_fusion = f32[2304,128]{1,0:T(8,128)S(1)} fusion(bf16[768,2304]{1,0:T(8,128)(2,1)} %param.7, bf16[768,256]{0,1:T(8,128)(2,1)S(1)} %all_gather.3, bf16[128,256]{1,0:T(8,128)(2,1)S(1)} %copy-done.3, f32[768]{0:T(1024)S(1)} %broadcast_add_fusion), kind=kOutput, calls=%fused_computation.1 | convolution fusion | flops 503513088 | bytes 5180416 | tf_op jit(solution)/shard_map/dot_general | solution.py:50
  88.2 15.0 %collective-permute-start.3 = (f32[768,128]{1,0:T(8,128)S(1)}, f32[768,128]{1,0:T(8,128)S(1)}, u32[]{:S(2)}, u32[]{:S(2)}) collective-permute-start(f32[768,128]{1,0:T(8,128)S(1)} %slice.15), channel_id=1, source_target_pairs={{0,1},{1,2},{2,3},{3,4},{4,5},{5,6},{6,7},{7,8},{8,9},{9,10},{10,1... | collective-permute-start | bytes 1179656 | tf_op jit(solution)/shard_map/ppermute | solution.py:23
  103.2 0.9 convolution_bitcast_fusion.1
  104.1 1.9 collective-permute-start.2
  106.0 0.9 fusion.10
  107.0 0.0 all-reduce.3.cloned.1.call-update
  107.0 185.8 %all-reduce.3.cloned.1.call-done = (f32[128,256]{0,1:T(8,128)}, f32[128,256]{1,0:T(8,128)}) async-done(((f32[128,256]{0,1:T(8,128)}, f32[128,256]{1,0:T(8,128)}), (f32[128,256]{0,1:T(8,128)}, f32[128,256]{1,0:T(8,128)})) %all-reduce.3.cloned.1.call-update) | async-done | bytes 262160 | tf_op jit(solution)/shard_map/psum | solution.py:61
  292.8 1.7 copy.12
  294.4 0.0 collective-permute-done.2
  294.4 0.0 collective-permute-done.3
  294.4 0.0 copy-done.4
  294.4 1.0 add_convert_fusion
  295.4 1.6 copy.17
  (3 shorter events, 0.1 us)
Async XLA Ops:
  7.2 17.5 %copy-start = (bf16[768,256]{1,0:T(8,128)(2,1)S(1)}, bf16[768,256]{1,0:T(8,128)(2,1)}, u32[]{:S(2)}) copy-start(bf16[768,256]{1,0:T(8,128)(2,1)} %param.11) | copy-start | bytes 1179652
  7.2 14.9 %copy-start.2 = (bf16[768,128]{1,0:T(8,128)(2,1)S(1)}, bf16[768,128]{1,0:T(8,128)(2,1)}, u32[]{:S(2)}) copy-start(bf16[768,128]{1,0:T(8,128)(2,1)} %param.6) | copy-start | bytes 589828
  7.2 56.9 %reduce-scatter.2.cloned.1.call-start = ((), (), s32[]{:S(2)}) async-start(), calls=%async_computation.1 | async-start | bytes 884736 | tf_op jit(solution)/shard_map/reduce_scatter | solution.py:39
  7.2 14.8 %copy-start.1 = (bf16[768,2304]{1,0:T(8,128)(2,1)S(1)}, bf16[768,2304]{1,0:T(8,128)(2,1)}, u32[]{:S(2)}) copy-start(bf16[768,2304]{1,0:T(8,128)(2,1)} %param.7) | copy-start | bytes 10616836
  7.2 14.8 %collective-permute-start.1 = (bf16[768,128]{1,0:T(8,128)(2,1)}, bf16[768,128]{1,0:T(8,128)(2,1)S(1)}, u32[]{:S(2)}, u32[]{:S(2)}) collective-permute-start(bf16[768,128]{1,0:T(8,128)(2,1)} %param.6), channel_id=1, source_target_pairs={{1,0},{2,1},{3,2},{4,3},{5,4},{6,5},{7,6},{8,7},{9,8},{10,9},{11,1... | collective-permute-start | bytes 589832 | tf_op jit(solution)/shard_map/ppermute | solution.py:15
  16.3 5.8 %collective-permute-start = (bf16[768,128]{1,0:T(8,128)(2,1)}, bf16[768,128]{1,0:T(8,128)(2,1)S(1)}, u32[]{:S(2)}, u32[]{:S(2)}) collective-permute-start(bf16[768,128]{1,0:T(8,128)(2,1)} %param.6), channel_id=1, source_target_pairs={{0,1},{1,2},{2,3},{3,4},{4,5},{5,6},{6,7},{7,8},{8,9},{9,10},{10,1... | collective-permute-start | bytes 589832 | tf_op jit(solution)/shard_map/ppermute | solution.py:14
  22.0 1.4 copy-start.3
  22.0 2.9 copy-start.5
  24.6 268.2 %all-reduce.3.cloned.1.call-start = ((), (), s32[]{:S(2)}) async-start(), calls=%async_computation.2 | async-start | bytes 524288 | tf_op jit(solution)/shard_map/psum | solution.py:61
  84.4 210.1 %copy-start.4 = (bf16[128,256]{1,0:T(8,128)(2,1)S(1)}, bf16[128,256]{1,0:T(8,128)(2,1)}, u32[]{:S(2)}) copy-start(bf16[128,256]{1,0:T(8,128)(2,1)} %param.8) | copy-start | bytes 196612
  88.2 206.2 %collective-permute-start.3 = (f32[768,128]{1,0:T(8,128)S(1)}, f32[768,128]{1,0:T(8,128)S(1)}, u32[]{:S(2)}, u32[]{:S(2)}) collective-permute-start(f32[768,128]{1,0:T(8,128)S(1)} %slice.15), channel_id=1, source_target_pairs={{0,1},{1,2},{2,3},{3,4},{4,5},{5,6},{6,7},{7,8},{8,9},{9,10},{10,1... | collective-permute-start | bytes 1179656 | tf_op jit(solution)/shard_map/ppermute | solution.py:23
  104.1 190.3 %collective-permute-start.2 = (bf16[768,128]{1,0:T(8,128)(2,1)S(1)}, bf16[768,128]{1,0:T(8,128)(2,1)S(1)}, u32[]{:S(2)}, u32[]{:S(2)}) collective-permute-start(bf16[768,128]{1,0:T(8,128)(2,1)S(1)} %slice.18), channel_id=1, source_target_pairs={{1,0},{2,1},{3,2},{4,3},{5,4},{6,5},{7,6},{8,7},{9,8},{10,9},{11,1... | collective-permute-start | bytes 589832 | tf_op jit(solution)/shard_map/ppermute | solution.py:23
Sparse Core Ops, SparseCore 0:
  24.7 39.3 reduce-scatter.1
  107.1 185.5 all-reduce.2
where the time goes:
time: 304 us
  waiting for transfers between devices  225 us (74%)
  starting transfers between devices  27.9 us (9%)
  blocking collectives  18.6 us (6%)
  between operations  14.2 us (5%)
  matrix products  10.3 us (3%)
  other arithmetic  4.16 us (1%)
  local copies, waits for them, and re-layouts  3.64 us (1%)
    psum x1, waiting for transfers between devices, body(): grad_self, grad_neigh = lax.psum((grad_self_part, grad_neigh_part), 'vert')  186 us
    reduce_scatter x1, waiting for transfers between devices, body(): lax.psum_scatter(partial_value, 'feat', scatter_dimension=1, tiled=True)  39.1 us
    all_gather x1, blocking collectives, body(): dpre = lax.all_gather(dpre_part, 'feat', axis=1, tiled=True)  18.6 us
    ppermute x2, starting transfers between devices, shifted(): return lax.ppermute(block, axis, route)  16.9 us
    ppermute x1, starting transfers between devices, extended(): after = lax.ppermute(leading, axis, down)  9.05 us
  transfers between devices with their start and end apart: 6, of which 2 were waited for; matrix products, arithmetic and copies ran while one was open for 3% of the time, Pallas kernels for 0%

commit v1 on v0

v1 whole, which is shorter than its diff:
```python
import jax
import jax.numpy as jnp
from jax import lax
from jax.sharding import Mesh, PartitionSpec as P

F32, BF16, F16 = jnp.float32, jnp.bfloat16, jnp.float16
Y, X, C = 8, 4, 2
VERT = ("y", "x", "c")


def contract(a, b, da, db):
    return lax.dot_general(a, b, (((da,), (db,)), ((), ())), preferred_element_type=F32)


def spread(block, axes, size):
    copies = jnp.broadcast_to(block[None], (size,) + block.shape)
    return lax.all_to_all(copies, axes, 0, 0, tiled=True)


def body(features, adjacency, w_self, w_neigh, bias, cotangent):
    rows, feats = features.shape
    hid = bias.shape[0]
    feat = lax.axis_size("z")
    width = hid // feat
    verts = Y * X * C
    up = [(i, i + 1) for i in range(verts - 1)]
    down = [(i + 1, i) for i in range(verts - 1)]

    before = lax.ppermute(features, VERT, up)
    after = lax.ppermute(features, VERT, down)
    deg = 1.0 + jnp.sum(adjacency.astype(F32), axis=1)
    window = jnp.concatenate([before, features, after], axis=0)
    agg = (contract(adjacency, window, 1, 0) / deg[:, None]).astype(BF16)
    partial = contract(w_self, features, 0, 1) + contract(w_neigh, agg, 0, 1)
    sent = (partial * 128.0).astype(F16).reshape(feat, width, rows)
    got = lax.all_to_all(sent, "z", 0, 0, tiled=True)
    offset = lax.axis_index("z") * width
    pre = jnp.sum(got.astype(F32), axis=0) * (1.0 / 128.0)
    pre = pre + lax.dynamic_slice_in_dim(bias, offset, width)[:, None]
    sig = jax.nn.sigmoid(pre)
    hidden = (pre * sig).astype(BF16).T

    upstream = lax.dynamic_slice_in_dim(cotangent, offset, width, 1).T.astype(F32)
    dpre_part = (upstream * sig * (1.0 + pre * (1.0 - sig))).astype(BF16)
    dpre = spread(dpre_part, "z", feat).reshape(hid, rows)

    grad = jnp.concatenate([contract(features, dpre, 0, 1), contract(agg, dpre, 0, 1)], axis=0)
    share = grad.shape[0] // (X * C)
    part = grad.astype(F16).reshape(X * C, share, hid)
    part = lax.all_to_all(part, ("x", "c"), 0, 0, tiled=True)
    part = jnp.sum(part.astype(F32), axis=0) * 0.25
    part = jnp.sum(spread(part.astype(F16), "y", Y).astype(F32), axis=0) * 0.125
    grad = spread(part.astype(F16), ("x", "c"), X * C).reshape(2 * feats, hid).astype(F32) * 32.0

    scaled = (contract(dpre, w_neigh, 0, 1) / deg[:, None]).astype(BF16)
    back = contract(adjacency, scaled, 0, 0)
    from_next = lax.ppermute((back[:rows] * 0.125).astype(F16), VERT, down)
    from_prev = lax.ppermute((back[2 * rows :] * 0.125).astype(F16), VERT, up)
    total = contract(dpre, w_self, 0, 1) + back[rows : 2 * rows]
    total = total + 8.0 * (from_next.astype(F32) + from_prev.astype(F32))
    return hidden, total.astype(BF16), grad[:feats], grad[feats:]


def solution(mesh):
    split = Mesh(mesh.devices.reshape(-1, Y, X, C), ("z",) + VERT)
    rows = P(VERT, None)
    return jax.shard_map(
        body,
        mesh=split,
        in_specs=(P(VERT, "z"), rows, P("z", None), P("z", None), P(), rows),
        out_specs=(P(VERT, "z"), P(VERT, "z"), P("z", None), P("z", None)),
        check_vma=False,
    )
```

time: 304 us -> 99.1 us (0.33)
  waiting for transfers between devices: 225 us -> 37.7 us
  blocking collectives: 18.6 us -> 0 us
  starting transfers between devices: 27.9 us -> 43.4 us
  between operations: 14.2 us -> 0.85 us
    psum x1 -> x0, waiting for transfers between devices: 186 us -> none  [body(): grad_self, grad_neigh = lax.psum((grad_self_part, grad_neigh_part), 'vert')]
    reduce_scatter x1 -> x0, waiting for transfers between devices: 39.1 us -> none  [body(): lax.psum_scatter(partial_value, 'feat', scatter_dimension=1, tiled=True)]
    all_to_all x0 -> x5, waiting for transfers between devices: none -> 37.6 us  [the longest x3 21.2 us: spread(): return lax.all_to_all(copies, axes, 0, 0, tiled=True)]
    all_to_all x0 -> x5, starting transfers between devices: none -> 27.3 us  [the longest x3 15.9 us: spread(): return lax.all_to_all(copies, axes, 0, 0, tiled=True)]
    all_gather x1 -> x0, blocking collectives: 18.6 us -> none  [body(): dpre = lax.all_gather(dpre_part, 'feat', axis=1, tiled=True)]
    ppermute x4, starting transfers between devices: 27.8 us -> 16.1 us  [the longest x1 9.05 us: body(): after = lax.ppermute(features, VERT, down)]
    unnamed x15 -> x13, local copies, waits for them, and re-layouts: 3.38 us -> 0.16 us
  transfers between devices with their start and end apart: 6 -> 9, of which waited for: 2 -> 5; matrix products, arithmetic and copies ran while one was open for 3% -> 11% of each run, Pallas kernels for 0% -> 0%
where the time goes in v1:
time: 99.1 us; the launch traced here: 98.4 us
  starting transfers between devices  43.4 us (44%)
  waiting for transfers between devices  37.7 us (38%)
  matrix products  9 us (9%)
  other arithmetic  4.3 us (4%)
  local copies, waits for them, and re-layouts  3.19 us (3%)
    all_to_all x3, waiting for transfers between devices, spread(): return lax.all_to_all(copies, axes, 0, 0, tiled=True)  21.2 us
    all_to_all x3, starting transfers between devices, spread(): return lax.all_to_all(copies, axes, 0, 0, tiled=True)  15.9 us
    all_to_all x1, waiting for transfers between devices, body(): got = lax.all_to_all(sent, 'z', 0, 0, tiled=True)  14.9 us
    ppermute x1, starting transfers between devices, body(): after = lax.ppermute(features, VERT, down)  9.05 us
    dot_general x7, matrix products, contract(): lax.dot_general(a, b, (((da,), (db,)), ((), ())), preferred_element_type=...  9 us
    all_to_all x1, starting transfers between devices, body(): got = lax.all_to_all(sent, 'z', 0, 0, tiled=True)  5.76 us
    all_to_all x1, starting transfers between devices, body(): part = lax.all_to_all(part, ('x', 'c'), 0, 0, tiled=True)  5.64 us
    ppermute x1, starting transfers between devices, body(): from_prev = lax.ppermute((back[2 * rows:] * 0.125).astype(F16), VERT, up)  3.22 us
  transfers between devices with their start and end apart: 9, of which 5 were waited for; matrix products, arithmetic and copies ran while one was open for 11% of the time, Pallas kernels for 0%

profile of v1, /device:TPU:1, one launch (start us, length us, event | category | flops | bytes accessed | tf_op | source)
XLA Modules:
  0.0 98.4 jit_solution(17826953750656454230)
XLA Ops:
  0.6 0.0 copy-start
  0.6 0.0 copy-start.2
  0.7 0.0 copy-start.1
  0.7 9.0 %collective-permute-start.1 = (bf16[768,128]{1,0:T(8,128)(2,1)}, bf16[768,128]{1,0:T(8,128)(2,1)S(1)}, u32[]{:S(2)}, u32[]{:S(2)}) collective-permute-start(bf16[768,128]{1,0:T(8,128)(2,1)} %param.6), channel_id=1, source_target_pairs={{1,0},{2,1},{3,2},{4,3},{5,4},{6,5},{7,6},{8,7},{9,8},{10,9},{11,1... | collective-permute-start | bytes 589832 | tf_op jit(solution)/shard_map/ppermute | solution.py:30
  9.7 1.9 %collective-permute-start = (bf16[768,128]{1,0:T(8,128)(2,1)}, bf16[768,128]{1,0:T(8,128)(2,1)S(1)}, u32[]{:S(2)}, u32[]{:S(2)}) collective-permute-start(bf16[768,128]{1,0:T(8,128)(2,1)} %param.6), channel_id=1, source_target_pairs={{0,1},{1,2},{2,3},{3,4},{4,5},{5,6},{6,7},{7,8},{8,9},{9,10},{10,1... | collective-permute-start | bytes 589832 | tf_op jit(solution)/shard_map/ppermute | solution.py:29
  11.7 1.3 %fusion.22 = f32[256,768]{1,0:T(8,128)S(1)} fusion(bf16[128,256]{1,0:T(8,128)(2,1)} %param.8, bf16[768,128]{1,0:T(8,128)(2,1)} %param.6), kind=kOutput, calls=%fused_computation.46 | convolution fusion | flops 50331648 | bytes 1048576 | tf_op jit(solution)/shard_map/dot_general | solution.py:12
  12.9 2.5 %convert_reduce_fusion = f32[768]{0:T(1024)S(1)} fusion(bf16[768,2304]{1,0:T(8,128)(2,1)} %param.7), kind=kLoop, calls=%fused_computation | loop fusion | flops 3538176 | bytes 3542016 | tf_op jit(solution)/shard_map/reduce_sum | solution.py:31
  15.5 0.0 copy-start.3
  15.5 0.0 copy-start.5
  15.5 0.0 collective-permute-done.1
  15.5 0.0 collective-permute-done
  15.5 0.0 copy-done.2
  15.5 0.0 copy-done.1
  15.5 1.3 %fusion.4 = bf16[128,768]{1,0:T(8,128)(2,1)S(1)} fusion(bf16[768,2304]{1,0:T(8,128)(2,1)S(1)} %copy-done.1, bf16[768,128]{1,0:T(8,128)(2,1)S(1)} %collective-permute-done.1, bf16[768,128]{1,0:T(8,128)(2,1)S(1)} %copy-done.2, bf16[768,128]{1,0:T(8,128)(2,1)S(1)} %collective-permute-done, f32[768]{0:T(1024)S(1)} %broadcast_add_fusion), kind=kOutput, calls=%fused_computation.10 | convolution fusion | flops 454950912 | bytes 4328448 | tf_op jit(solution)/shard_map/dot_general | solution.py:12
  16.8 0.0 copy-done.3
  16.9 1.1 %fusion.2 = f16[256,768]{1,0:T(8,128)(2,1)} fusion(f32[256,768]{1,0:T(8,128)S(1)} %fusion.22, bf16[128,768]{1,0:T(8,128)(2,1)S(1)} %fusion.4, bf16[128,256]{1,0:T(8,128)(2,1)S(1)} %copy-done.3), kind=kOutput, calls=%fused_computation.5 | convolution fusion | flops 50921472 | bytes 1441792 | tf_op jit(solution)/shard_map/dot_general | solution.py:12
  17.9 5.8 %all-to-all-start = ((f16[8,32,768]{2,1,0:T(8,128)(2,1)}), f16[8,32,768]{2,1,0:T(8,128)(2,1)S(1)}, u32[]{:S(2)}, u32[]{:S(2)}) async-start(f16[8,32,768]{2,1,0:T(8,128)(2,1)} %bitcast.1), calls=%async_computation | async-start | bytes 786432 | tf_op jit(solution)/shard_map/all_to_all | solution.py:36
  23.7 0.0 copy-done.5
  23.7 0.1 dynamic_slice.6
  23.7 0.0 copy-done
  23.7 0.1 constant_dynamic-slice_fusion
  23.9 0.1 copy.15
  24.0 14.9 %all-to-all-done = f16[8,32,768]{2,1,0:T(8,128)(2,1)S(1)} async-done(((f16[8,32,768]{2,1,0:T(8,128)(2,1)}), f16[8,32,768]{2,1,0:T(8,128)(2,1)S(1)}, u32[]{:S(2)}, u32[]{:S(2)}) %all-to-all-start) | async-done | bytes 393248 | tf_op jit(solution)/shard_map/all_to_all | solution.py:36
  38.9 0.1 convert_reduce_fusion.1
  39.0 0.1 fusion.15
  39.1 0.8 broadcast_in_dim.6
  39.9 3.5 %all-to-all-start.1 = ((bf16[8,32,768]{2,1,0:T(8,128)(2,1)}), bf16[8,32,768]{2,1,0:T(8,128)(2,1)S(1)}, u32[]{:S(2)}, u32[]{:S(2)}) async-start(bf16[8,32,768]{2,1,0:T(8,128)(2,1)} %broadcast_in_dim.6), calls=%async_computation.1 | async-start | bytes 786432 | tf_op jit(solution)/shard_map/all_to_all | solution.py:17
  43.4 0.7 fusion.19
  44.1 14.3 %all-to-all-done.1 = bf16[8,32,768]{2,1,0:T(8,128)(2,1)S(1)} async-done(((bf16[8,32,768]{2,1,0:T(8,128)(2,1)}), bf16[8,32,768]{2,1,0:T(8,128)(2,1)S(1)}, u32[]{:S(2)}, u32[]{:S(2)}) %all-to-all-start.1) | async-done | bytes 393248 | tf_op jit(solution)/shard_map/all_to_all | solution.py:17
  58.4 0.3 convolution_convert_fusion
  58.7 0.3 fusion.5
  59.0 0.7 pad_maximum_fusion
  59.7 5.6 %all-to-all-start.2 = ((f16[8,32,256]{2,1,0:T(8,128)(2,1)}), f16[8,32,256]{2,1,0:T(8,128)(2,1)S(1)}, u32[]{:S(2)}, u32[]{:S(2)}) async-start(f16[8,32,256]{2,1,0:T(8,128)(2,1)} %bitcast.7), calls=%async_computation.2 | async-start | bytes 262144 | tf_op jit(solution)/shard_map/all_to_all | solution.py:50
  65.4 3.8 %convolution_bitcast_fusion = f32[2304,128]{1,0:T(8,128)S(1)} fusion(bf16[768,2304]{1,0:T(8,128)(2,1)} %param.7, bf16[256,768]{1,0:T(8,128)(2,1)S(1)} %bitcast.52, bf16[128,256]{1,0:T(8,128)(2,1)S(1)} %copy-done.3, f32[768]{0:T(1024)S(1)} %broadcast_add_fusion), kind=kOutput, calls=%fused_computation.1 | convolution fusion | flops 503513088 | bytes 5180416 | tf_op jit(solution)/shard_map/dot_general | solution.py:12
  69.2 1.5 %all-to-all-done.2 = f16[8,32,256]{2,1,0:T(8,128)(2,1)S(1)} async-done(((f16[8,32,256]{2,1,0:T(8,128)(2,1)}), f16[8,32,256]{2,1,0:T(8,128)(2,1)S(1)}, u32[]{:S(2)}, u32[]{:S(2)}) %all-to-all-start.2) | async-done | bytes 131104 | tf_op jit(solution)/shard_map/all_to_all | solution.py:50
  70.7 0.7 broadcast_in_dim.7
  71.3 6.8 %all-to-all-start.3 = ((f16[8,32,256]{2,1,0:T(8,128)(2,1)}), f16[8,32,256]{2,1,0:T(8,128)(2,1)S(1)}, u32[]{:S(2)}, u32[]{:S(2)}) async-start(f16[8,32,256]{2,1,0:T(8,128)(2,1)} %broadcast_in_dim.7), calls=%async_computation.3 | async-start | bytes 262144 | tf_op jit(solution)/shard_map/all_to_all | solution.py:17
  78.2 0.1 fusion.12
  78.2 3.2 %collective-permute-start.3 = (f16[768,128]{1,0:T(8,128)(2,1)S(1)}, f16[768,128]{1,0:T(8,128)(2,1)S(1)}, u32[]{:S(2)}, u32[]{:S(2)}) collective-permute-start(f16[768,128]{1,0:T(8,128)(2,1)S(1)} %get-tuple-element.5), channel_id=1, source_target_pairs={{0,1},{1,2},{2,3},{3,4},{4,5},{5,6},{6,7},{7,8},{8,9},{9,10},{10,1... | collective-permute-start | bytes 589832 | tf_op jit(solution)/shard_map/ppermute | solution.py:58
  81.5 1.9 %collective-permute-start.2 = (f16[768,128]{1,0:T(8,128)(2,1)S(1)}, f16[768,128]{1,0:T(8,128)(2,1)S(1)}, u32[]{:S(2)}, u32[]{:S(2)}) collective-permute-start(f16[768,128]{1,0:T(8,128)(2,1)S(1)} %get-tuple-element.4), channel_id=1, source_target_pairs={{1,0},{2,1},{3,2},{4,3},{5,4},{6,5},{7,6},{8,7},{9,8},{10,9},{11,1... | collective-permute-start | bytes 589832 | tf_op jit(solution)/shard_map/ppermute | solution.py:57
  83.4 2.6 %all-to-all-done.3 = f16[8,32,256]{2,1,0:T(8,128)(2,1)S(1)} async-done(((f16[8,32,256]{2,1,0:T(8,128)(2,1)}), f16[8,32,256]{2,1,0:T(8,128)(2,1)S(1)}, u32[]{:S(2)}, u32[]{:S(2)}) %all-to-all-start.3) | async-done | bytes 131104 | tf_op jit(solution)/shard_map/all_to_all | solution.py:17
  86.1 0.7 broadcast_in_dim.8
  86.7 5.6 %all-to-all-start.4 = ((f16[8,32,256]{2,1,0:T(8,128)(2,1)}), f16[8,32,256]{2,1,0:T(8,128)(2,1)S(1)}, u32[]{:S(2)}, u32[]{:S(2)}) async-start(f16[8,32,256]{2,1,0:T(8,128)(2,1)} %broadcast_in_dim.8), calls=%async_computation.4 | async-start | bytes 262144 | tf_op jit(solution)/shard_map/all_to_all | solution.py:17
  92.4 0.0 collective-permute-done.3
  92.4 0.0 collective-permute-done.2
  92.4 1.0 %add_convert_fusion = bf16[768,128]{1,0:T(8,128)(2,1)} fusion(f16[768,128]{1,0:T(8,128)(2,1)S(1)} %collective-permute-done.3, f16[768,128]{1,0:T(8,128)(2,1)S(1)} %collective-permute-done.2, f32[2304,128]{1,0:T(8,128)S(1)} %convolution_bitcast_fusion, bf16[256,768]{1,0:T(8,128)(2,1)S(1)} %bitcast.53, bf16[128,256]{1,0:T(8,128)(2,1)S(1)} %copy-done.4), kind=kOutput, calls=%fused_computation.24 | convolution fusion | flops 51019776 | bytes 1441792 | tf_op jit(solution)/shard_map/dot_general | solution.py:12
  93.4 4.3 %all-to-all-done.4 = f16[8,32,256]{2,1,0:T(8,128)(2,1)S(1)} async-done(((f16[8,32,256]{2,1,0:T(8,128)(2,1)}), f16[8,32,256]{2,1,0:T(8,128)(2,1)S(1)}, u32[]{:S(2)}, u32[]{:S(2)}) %all-to-all-start.4) | async-done | bytes 131104 | tf_op jit(solution)/shard_map/all_to_all | solution.py:17
  97.7 0.7 fusion.21
  (8 shorter events, 0.1 us)
Async XLA Ops:
  0.6 23.1 %copy-start = (bf16[768,256]{1,0:T(8,128)(2,1)S(1)}, bf16[768,256]{1,0:T(8,128)(2,1)}, u32[]{:S(2)}) copy-start(bf16[768,256]{1,0:T(8,128)(2,1)} %param.11) | copy-start | bytes 1179652
  0.6 14.9 %copy-start.2 = (bf16[768,128]{1,0:T(8,128)(2,1)S(1)}, bf16[768,128]{1,0:T(8,128)(2,1)}, u32[]{:S(2)}) copy-start(bf16[768,128]{1,0:T(8,128)(2,1)} %param.6) | copy-start | bytes 589828
  0.7 14.9 %copy-start.1 = (bf16[768,2304]{1,0:T(8,128)(2,1)S(1)}, bf16[768,2304]{1,0:T(8,128)(2,1)}, u32[]{:S(2)}) copy-start(bf16[768,2304]{1,0:T(8,128)(2,1)} %param.7) | copy-start | bytes 10616836
  0.7 14.8 %collective-permute-start.1 = (bf16[768,128]{1,0:T(8,128)(2,1)}, bf16[768,128]{1,0:T(8,128)(2,1)S(1)}, u32[]{:S(2)}, u32[]{:S(2)}) collective-permute-start(bf16[768,128]{1,0:T(8,128)(2,1)} %param.6), channel_id=1, source_target_pairs={{1,0},{2,1},{3,2},{4,3},{5,4},{6,5},{7,6},{8,7},{9,8},{10,9},{11,1... | collective-permute-start | bytes 589832 | tf_op jit(solution)/shard_map/ppermute | solution.py:30
  9.7 5.8 %collective-permute-start = (bf16[768,128]{1,0:T(8,128)(2,1)}, bf16[768,128]{1,0:T(8,128)(2,1)S(1)}, u32[]{:S(2)}, u32[]{:S(2)}) collective-permute-start(bf16[768,128]{1,0:T(8,128)(2,1)} %param.6), channel_id=1, source_target_pairs={{0,1},{1,2},{2,3},{3,4},{4,5},{5,6},{6,7},{7,8},{8,9},{9,10},{10,1... | collective-permute-start | bytes 589832 | tf_op jit(solution)/shard_map/ppermute | solution.py:29
  15.5 1.4 %copy-start.3 = (bf16[128,256]{1,0:T(8,128)(2,1)S(1)}, bf16[128,256]{1,0:T(8,128)(2,1)}, u32[]{:S(2)}) copy-start(bf16[128,256]{1,0:T(8,128)(2,1)} %param.9) | copy-start | bytes 196612
  15.5 8.2 %copy-start.5 = (f32[256]{0:T(256)S(1)}, f32[256]{0:T(256)}, u32[]{:S(2)}) copy-start(f32[256]{0:T(256)} %param.10) | copy-start | bytes 3076
  17.9 21.0 %all-to-all-start = ((f16[8,32,768]{2,1,0:T(8,128)(2,1)}), f16[8,32,768]{2,1,0:T(8,128)(2,1)S(1)}, u32[]{:S(2)}, u32[]{:S(2)}) async-start(f16[8,32,768]{2,1,0:T(8,128)(2,1)} %bitcast.1), calls=%async_computation | async-start | bytes 786432 | tf_op jit(solution)/shard_map/all_to_all | solution.py:36
  39.9 18.5 %all-to-all-start.1 = ((bf16[8,32,768]{2,1,0:T(8,128)(2,1)}), bf16[8,32,768]{2,1,0:T(8,128)(2,1)S(1)}, u32[]{:S(2)}, u32[]{:S(2)}) async-start(bf16[8,32,768]{2,1,0:T(8,128)(2,1)} %broadcast_in_dim.6), calls=%async_computation.1 | async-start | bytes 786432 | tf_op jit(solution)/shard_map/all_to_all | solution.py:17
  59.7 10.9 %all-to-all-start.2 = ((f16[8,32,256]{2,1,0:T(8,128)(2,1)}), f16[8,32,256]{2,1,0:T(8,128)(2,1)S(1)}, u32[]{:S(2)}, u32[]{:S(2)}) async-start(f16[8,32,256]{2,1,0:T(8,128)(2,1)} %bitcast.7), calls=%async_computation.2 | async-start | bytes 262144 | tf_op jit(solution)/shard_map/all_to_all | solution.py:50
  65.3 27.0 %copy-start.4 = (bf16[128,256]{1,0:T(8,128)(2,1)S(1)}, bf16[128,256]{1,0:T(8,128)(2,1)}, u32[]{:S(2)}) copy-start(bf16[128,256]{1,0:T(8,128)(2,1)} %param.8) | copy-start | bytes 196612
  71.3 14.7 %all-to-all-start.3 = ((f16[8,32,256]{2,1,0:T(8,128)(2,1)}), f16[8,32,256]{2,1,0:T(8,128)(2,1)S(1)}, u32[]{:S(2)}, u32[]{:S(2)}) async-start(f16[8,32,256]{2,1,0:T(8,128)(2,1)} %broadcast_in_dim.7), calls=%async_computation.3 | async-start | bytes 262144 | tf_op jit(solution)/shard_map/all_to_all | solution.py:17
  78.2 14.1 %collective-permute-start.3 = (f16[768,128]{1,0:T(8,128)(2,1)S(1)}, f16[768,128]{1,0:T(8,128)(2,1)S(1)}, u32[]{:S(2)}, u32[]{:S(2)}) collective-permute-start(f16[768,128]{1,0:T(8,128)(2,1)S(1)} %get-tuple-element.5), channel_id=1, source_target_pairs={{0,1},{1,2},{2,3},{3,4},{4,5},{5,6},{6,7},{7,8},{8,9},{9,10},{10,1... | collective-permute-start | bytes 589832 | tf_op jit(solution)/shard_map/ppermute | solution.py:58
  81.5 10.9 %collective-permute-start.2 = (f16[768,128]{1,0:T(8,128)(2,1)S(1)}, f16[768,128]{1,0:T(8,128)(2,1)S(1)}, u32[]{:S(2)}, u32[]{:S(2)}) collective-permute-start(f16[768,128]{1,0:T(8,128)(2,1)S(1)} %get-tuple-element.4), channel_id=1, source_target_pairs={{1,0},{2,1},{3,2},{4,3},{5,4},{6,5},{7,6},{8,7},{9,8},{10,9},{11,1... | collective-permute-start | bytes 589832 | tf_op jit(solution)/shard_map/ppermute | solution.py:57
  86.7 10.9 %all-to-all-start.4 = ((f16[8,32,256]{2,1,0:T(8,128)(2,1)}), f16[8,32,256]{2,1,0:T(8,128)(2,1)S(1)}, u32[]{:S(2)}, u32[]{:S(2)}) async-start(f16[8,32,256]{2,1,0:T(8,128)(2,1)} %broadcast_in_dim.8), calls=%async_computation.4 | async-start | bytes 262144 | tf_op jit(solution)/shard_map/all_to_all | solution.py:17

commit v2 on v1

v2 whole, which is shorter than its diff:
```python
import jax
import jax.numpy as jnp
from jax import lax
from jax.experimental import pallas as pl
from jax.experimental.pallas import tpu as pltpu
from jax.sharding import Mesh, PartitionSpec as P

F32, BF16, F16 = jnp.float32, jnp.bfloat16, jnp.float16
Y, X, C = 8, 4, 2
VERT = ("y", "x", "c")
PARAMS = pltpu.CompilerParams(vmem_limit_bytes=16 * 1024 * 1024)
VMEM = pl.BlockSpec()
SMEM = pl.BlockSpec(memory_space=pltpu.SMEM)


def contract(a, b, da, db):
    return lax.dot_general(a, b, (((da,), (db,)), ((), ())), preferred_element_type=F32)


def mm(a, b):
    return jnp.dot(a, b, preferred_element_type=F32)


def exchange(blocks, axes):
    return lax.all_to_all(blocks, axes, 0, 0, tiled=True)


def exchange_down(blocks, axes):
    return lax.all_to_all(blocks, axes, 0, 0, tiled=True, axis_index_groups=[list(range(7, -1, -1))])


def swap_cores(block):
    return lax.ppermute(block, "c", [(0, 1), (1, 0)])


def swap_chips(block):
    pairs = [(i, i + 1) for i in range(1, Y * X * C - 1, 2)]
    return lax.ppermute(block, VERT, pairs + [(j, i) for i, j in pairs])


def side_kernel(even_ref, side_ref):
    side_ref[0] = even_ref[0]


def own_kernel(adj_ref, x_ref, ws_ref, wn_ref, own_ref, w_ref, wt_ref):
    rows = x_ref.shape[0]
    x = x_ref[...]
    wide = jnp.concatenate([x, jnp.ones_like(x)], axis=1)
    own_ref[...] = mm(adj_ref[:, rows : 2 * rows], wide)
    w = jnp.concatenate([ws_ref[...], wn_ref[...]], axis=0)
    w_ref[...] = w
    wt_ref[...] = w.T


def agg_kernel(even_ref, adj_ref, far_ref, near_ref, own_ref, x_ref, wt_ref, both_ref, deg_ref, part_ref):
    rows, feats = x_ref.shape
    even = even_ref[0] == 1
    far, near = far_ref[...], near_ref[...]
    ones = jnp.ones_like(far)
    before = jnp.concatenate([jnp.where(even, far, near), ones], axis=1)
    after = jnp.concatenate([jnp.where(even, near, far), ones], axis=1)
    total = own_ref[...] + mm(adj_ref[:, :rows], before) + mm(adj_ref[:, 2 * rows :], after)
    deg = 1.0 + total[:, feats:]
    deg_ref[...] = deg
    agg = (total[:, :feats] / deg).astype(BF16)
    both = jnp.concatenate([x_ref[...], agg], axis=1).T
    both_ref[...] = both
    part_ref[...] = mm(wt_ref[...], both) * 128.0


def act_kernel(pre_ref, bias_ref, up_ref, hidden_ref, dpre_ref):
    pre = pre_ref[...] * (1.0 / 128.0) + bias_ref[:, :1]
    sig = jax.nn.sigmoid(pre)
    hidden_ref[...] = pre * sig
    dpre = (up_ref[...].astype(F32) * sig * (1.0 + pre * (1.0 - sig))).astype(BF16)
    for i in range(dpre_ref.shape[0]):
        dpre_ref[i] = dpre


def gathered(ref):
    size = ref.shape[0] // 8
    return jnp.concatenate([ref[i * size : (i + 1) * size] for i in range(7, -1, -1)], axis=0)


def grad_kernel(both_ref, dpre_ref, grad_ref):
    grad_ref[...] = contract(both_ref[...], gathered(dpre_ref), 1, 1)


def back_kernel(adj_ref, deg_ref, w_ref, dpre_ref, first_ref, mid_ref, last_ref):
    rows, feats = mid_ref.shape
    dpre = gathered(dpre_ref)
    scaled = (mm(w_ref[feats:], dpre) / deg_ref[...]).astype(BF16)
    first_ref[...] = mm(scaled, adj_ref[:, :rows]).T
    last_ref[...] = mm(scaled, adj_ref[:, 2 * rows :]).T
    mid_ref[...] = (mm(scaled, adj_ref[:, rows : 2 * rows]) + mm(w_ref[:feats], dpre)).T


def cost(us):
    return pl.CostEstimate(flops=int(us * 1e9), bytes_accessed=0, transcendentals=0)


def body(features, adjacency, w_self, w_neigh, bias, cotangent):
    rows, feats = features.shape
    hid = bias.shape[0]
    feat = lax.axis_size("z")
    width = hid // feat
    even = lax.axis_index("c") == 0
    shape = jax.ShapeDtypeStruct

    far = swap_chips(features)
    near = swap_cores(features)
    side = pl.pallas_call(
        side_kernel,
        in_specs=[SMEM],
        out_specs=SMEM,
        out_shape=shape((1,), jnp.int32),
        cost_estimate=cost(5),
    )(even.astype(jnp.int32).reshape(1))
    own, w_both, w_flip = pl.pallas_call(
        own_kernel,
        in_specs=[VMEM] * 4,
        out_specs=[VMEM] * 3,
        out_shape=[shape((rows, 2 * feats), F32), shape((2 * feats, hid), BF16), shape((hid, 2 * feats), BF16)],
        compiler_params=PARAMS,
        cost_estimate=cost(3),
    )(adjacency, features, w_self, w_neigh)
    both, deg, part = pl.pallas_call(
        agg_kernel,
        in_specs=[SMEM] + [VMEM] * 6,
        out_specs=[VMEM] * 3,
        out_shape=[shape((2 * feats, rows), BF16), shape((rows, feats), F32), shape((hid, rows), F32)],
        compiler_params=PARAMS,
        cost_estimate=cost(3),
    )(side, adjacency, far, near, own, features, w_flip)
    offset = lax.axis_index("z") * width
    bias_part = jnp.broadcast_to(lax.dynamic_slice_in_dim(bias, offset, width)[:, None], (width, 128))
    upstream = lax.dynamic_slice_in_dim(cotangent, offset, width, 1).T
    deg = deg[:, 0][None]
    sent = part.astype(F16).reshape(feat, width, rows)
    sent, deg, upstream, bias_part = lax.optimization_barrier((sent, deg, upstream, bias_part))
    got = jnp.sum(exchange(sent, "z").astype(F32), axis=0)
    hidden, dpre = pl.pallas_call(
        act_kernel,
        in_specs=[VMEM] * 3,
        out_specs=[VMEM] * 2,
        out_shape=[shape((width, rows), F32), shape((feat, width, rows), BF16)],
        compiler_params=PARAMS,
        cost_estimate=cost(1),
    )(got, bias_part, upstream)
    dpre, hidden = lax.optimization_barrier((exchange_down(dpre, "z"), hidden))
    dpre = dpre.reshape(hid, rows)

    grad = pl.pallas_call(
        grad_kernel,
        in_specs=[VMEM] * 2,
        out_specs=VMEM,
        out_shape=shape((2 * feats, hid), F32),
        compiler_params=PARAMS,
        cost_estimate=cost(1),
    )(both, dpre)
    share = 2 * feats // (X * C)
    piece = grad.astype(F16).reshape(X * C, share, hid)
    piece = exchange_down(piece, ("x", "c"))
    piece = jnp.broadcast_to((jnp.sum(piece.astype(F32), axis=0) * 0.25).astype(F16), (Y, share, hid))
    piece = exchange_down(piece, "y")

    first, mid, last = pl.pallas_call(
        back_kernel,
        in_specs=[VMEM] * 4,
        out_specs=[VMEM] * 3,
        out_shape=[shape((rows, feats), F32)] * 3,
        compiler_params=PARAMS,
        cost_estimate=pl.CostEstimate(flops=6 * rows * rows * feats, bytes_accessed=6 * rows * rows, transcendentals=0),
    )(adjacency, deg, w_both, dpre)
    first = (first * 0.125).astype(F16)
    last = (last * 0.125).astype(F16)
    from_far = swap_chips(jnp.where(even, first, last))
    near = jnp.where(even, last, first)
    piece, near = lax.optimization_barrier((piece, near))
    piece = jnp.broadcast_to((jnp.sum(piece.astype(F32), axis=0) * 0.125).astype(F16), (X * C, share, hid))
    from_near = swap_cores(near)
    grad = exchange_down(piece, ("x", "c")).reshape(2 * feats, hid).astype(F32) * 32.0
    total = mid + 8.0 * (from_far.astype(F32) + from_near.astype(F32))
    return hidden.astype(BF16).T, total.astype(BF16), grad[:feats], grad[feats:]


def solution(mesh):
    split = Mesh(mesh.devices.reshape(-1, Y, X, C), ("z",) + VERT)
    rows = P(VERT, None)
    return jax.shard_map(
        body,
        mesh=split,
        in_specs=(P(VERT, "z"), rows, P("z", None), P("z", None), P(), rows),
        out_specs=(P(VERT, "z"), P(VERT, "z"), P("z", None), P("z", None)),
        check_vma=False,
    )
```

time: 99.1 us -> 90 us (0.908)
  waiting for transfers between devices: 37.7 us -> 2.53 us
  blocking collectives: 0 us -> 31.4 us
  matrix products: 9 us -> 0 us
  local copies, waits for them, and re-layouts: 3.19 us -> 8.21 us
  Pallas kernels: 0 us -> 4.12 us
  starting transfers between devices: 43.4 us -> 39.9 us
  other arithmetic: 4.3 us -> 2.34 us
    all_to_all x5 -> x3, waiting for transfers between devices: 37.6 us -> 2.52 us  [exchange_down(): lax.all_to_all(blocks, axes, 0, 0, tiled=True, axis_index_groups=[list(ra...]
    all_to_all x0 -> x2, blocking collectives: none -> 31.4 us  [the longest x1 20.3 us: exchange(): return lax.all_to_all(blocks, axes, 0, 0, tiled=True)]
    dot_general x7 -> x0, matrix products: 9 us -> none  [contract(): lax.dot_general(a, b, (((da,), (db,)), ((), ())), preferred_element_type=...]
    unnamed x13 -> x17, local copies, waits for them, and re-layouts: 0.16 us -> 5.7 us
    pallas_call x0 -> x6, Pallas kernels: none -> 4.12 us  [the longest x1 1.78 us: body(): pl.pallas_call(agg_kernel, in_specs=[SMEM] + [VMEM] * 6, out_specs=[VMEM]...]
    all_to_all x5 -> x3, starting transfers between devices: 27.3 us -> 24.7 us  [exchange_down(): lax.all_to_all(blocks, axes, 0, 0, tiled=True, axis_index_groups=[list(ra...]
    reduce_sum x4 -> x3, other arithmetic: 2.63 us -> 0.1 us  [the longest x1 0.05 us: body(): got = jnp.sum(exchange(sent, 'z').astype(F32), axis=0)]
  transfers between devices with their start and end apart: 9 -> 7, of which waited for: 5 -> 3; matrix products, arithmetic and copies ran while one was open for 11% -> 3% of each run, Pallas kernels for 0% -> 2%
where the time goes in v2:
time: 90 us; the launch traced here: 89.3 us
  starting transfers between devices  39.9 us (44%)
  blocking collectives  31.4 us (35%)
  local copies, waits for them, and re-layouts  8.21 us (9%)
  Pallas kernels  4.12 us (5%)
  waiting for transfers between devices  2.53 us (3%)
  other arithmetic  2.34 us (3%)
    all_to_all x3, starting transfers between devices, exchange_down(): lax.all_to_all(blocks, axes, 0, 0, tiled=True, axis_index_groups=[list(ra...  24.7 us
    all_to_all x1, blocking collectives, exchange(): return lax.all_to_all(blocks, axes, 0, 0, tiled=True)  20.3 us
    all_to_all x1, blocking collectives, exchange_down(): lax.all_to_all(blocks, axes, 0, 0, tiled=True, axis_index_groups=[list(ra...  11.1 us
    ppermute x2, starting transfers between devices, swap_chips(): return lax.ppermute(block, VERT, pairs + [(j, i) for i, j in pairs])  7.92 us
    ppermute x2, starting transfers between devices, swap_cores(): return lax.ppermute(block, 'c', [(0, 1), (1, 0)])  7.28 us
    unnamed x17, local copies, waits for them, and re-layouts  5.7 us
    all_to_all x3, waiting for transfers between devices, exchange_down(): lax.all_to_all(blocks, axes, 0, 0, tiled=True, axis_index_groups=[list(ra...  2.52 us
  transfers between devices with their start and end apart: 7, of which 3 were waited for; matrix products, arithmetic and copies ran while one was open for 3% of the time, Pallas kernels for 2%

profile of v2, /device:TPU:1, one launch (start us, length us, event | category | flops | bytes accessed | tf_op | source)
XLA Modules:
  0.0 89.3 jit_solution(12414438906193191261)
XLA Ops:
  0.6 0.0 copy-start
  0.6 4.6 %collective-permute-start = (bf16[768,128]{1,0:T(8,128)(2,1)}, bf16[768,128]{1,0:T(8,128)(2,1)S(1)}, u32[]{:S(2)}, u32[]{:S(2)}) collective-permute-start(bf16[768,128]{1,0:T(8,128)(2,1)} %x_ref.3), channel_id=1, source_target_pairs={{1,2},{3,4},{5,6},{7,8},{9,10},{11,12},{13,14},{15,16},{17,18},{19... | collective-permute-start | bytes 589832 | tf_op jit(solution)/shard_map/ppermute | solution.py:38
  5.3 5.0 %collective-permute-start.1 = (bf16[768,128]{1,0:T(8,128)(2,1)}, bf16[768,128]{1,0:T(8,128)(2,1)S(1)}, u32[]{:S(2)}, u32[]{:S(2)}) collective-permute-start(bf16[768,128]{1,0:T(8,128)(2,1)} %x_ref.3), channel_id=1, source_target_pairs={{0,1},{1,0},{2,3},{3,2},{4,5},{5,4},{6,7},{7,6},{8,9},{9,8},{10,11... | collective-permute-start | bytes 589832 | tf_op jit(solution)/shard_map/ppermute | solution.py:33
  10.3 0.0 copy-start.7
  10.3 0.0 copy-start.4
  10.3 0.0 copy-start.5
  10.3 0.0 copy-start.6
  10.3 0.5 shard_map.93.even_ref
  10.8 0.0 copy-done
  10.8 0.1 constant_dynamic-slice_fusion
  11.0 0.1 copy.13
  11.1 0.0 copy-done.7
  11.1 0.1 dynamic_slice.7
  11.2 0.0 copy-done.4
  11.2 0.0 copy-done.5
  11.2 0.0 copy-done.6
  11.2 2.0 %copy-done.1 = bf16[768,2304]{1,0:T(8,128)(2,1)S(1)} copy-done((bf16[768,2304]{1,0:T(8,128)(2,1)S(1)}, bf16[768,2304]{1,0:T(8,128)(2,1)}, u32[]{:S(2)}) %copy-start.1) | copy-done | bytes 3538968
  13.2 0.5 shard_map.94
  13.7 0.0 collective-permute-done.far_ref
  13.7 0.0 collective-permute-done.1.near_ref
  13.7 1.5 %copy-done.2 = bf16[768,2304]{1,0:T(8,128)(2,1)S(1)} copy-done((bf16[768,2304]{1,0:T(8,128)(2,1)S(1)}, bf16[768,2304]{1,0:T(8,128)(2,1)}, u32[]{:S(2)}) %copy-start.2) | copy-done | bytes 3538968
  15.2 1.8 %shard_map.95 = (bf16[256,768]{1,0:T(8,128)(2,1)S(1)}, f32[768,128]{1,0:T(8,128)S(1)}, f32[256,768]{1,0:T(8,128)S(1)}) custom-call(s32[1]{0:T(128)} %shard_map.93.even_ref, bf16[768,2304]{1,0:T(8,128)(2,1)S(1)} %copy-done.2, bf16[768,128]{1,0:T(8,128)(2,1)S(1)} %collective-permute-done.far_ref, bf16[768,128]{1,0:T(8,128)(2,1)S(1)} %collective-permute-done.1.near_ref, ...), custom_call_target="tpu_custom_call" | custom-call | flops 3000000000 | tf_op jit(solution)/shard_map/pallas_call | solution.py:127
  17.1 0.2 slice_reduce_fusion
  17.3 0.1 broadcast_in_dim.12.bias_ref
  17.3 20.3 %all_to_all.25 = f16[8,32,768]{2,1,0:T(8,128)(2,1)S(1)} all-to-all(f16[8,32,768]{2,1,0:T(8,128)(2,1)S(1)} %bitcast.12), channel_id=1, replica_groups=mesh['z'=8,'y'=8,'x'=4,'c'=2] {'z'}, dimensions={0} | all-to-all | bytes 786432 | tf_op jit(solution)/shard_map/all_to_all | solution.py:25
  37.6 0.1 convert_reduce_fusion.pre_ref
  37.7 0.1 shard_map.96
  37.8 11.1 %all_to_all.26 = bf16[8,32,768]{2,1,0:T(8,128)(2,1)S(1)} all-to-all(bf16[8,32,768]{2,1,0:T(8,128)(2,1)S(1)} %get-tuple-element.30), channel_id=1, replica_groups={{448,384,320,256,192,128,64,0},{449,385,321,257,193,129,65,1},{450,386,..., dimensions={0} | all-to-all | bytes 786432 | tf_op jit(solution)/shard_map/all_to_all | solution.py:29
  48.9 0.3 shard_map.98
  49.2 0.7 convert_element_type.50
  49.9 9.3 %all-to-all-start.2 = ((f16[8,32,256]{2,1,0:T(8,128)(2,1)}), f16[8,32,256]{2,1,0:T(8,128)(2,1)S(1)}, u32[]{:S(2)}, u32[]{:S(2)}) async-start(f16[8,32,256]{2,1,0:T(8,128)(2,1)} %bitcast.5), calls=%async_computation.2 | async-start | bytes 262144 | tf_op jit(solution)/shard_map/all_to_all | solution.py:29
  59.2 2.0 %copy-done.3 = bf16[768,2304]{1,0:T(8,128)(2,1)S(1)} copy-done((bf16[768,2304]{1,0:T(8,128)(2,1)S(1)}, bf16[768,2304]{1,0:T(8,128)(2,1)}, u32[]{:S(2)}) %copy-start.3) | copy-done | bytes 3538968
  61.2 0.9 %shard_map.97 = (f32[768,128]{1,0:T(8,128)S(1)}, f32[768,128]{1,0:T(8,128)S(1)}, f32[768,128]{1,0:T(8,128)S(1)}) custom-call(bf16[768,2304]{1,0:T(8,128)(2,1)S(1)} %copy-done.3, f32[1,768]{1,0:T(1,128)S(1)} %broadcast_in_dim_squeeze.3.deg_ref, bf16[256,256]{1,0:T(8,128)(2,1)S(1)} %get-tuple-element.34.w_ref, bf16[256,768]{1,0:T(8,128)(2,1)S(1)} %bitcast.10), custom_call_target="tpu_custom_call" | custom-call | flops 452984832 | bytes 3538944 | tf_op jit(solution)/shard_map/pallas_call | solution.py:167
  62.1 0.3 all-to-all-done.2
  62.5 0.7 broadcast_in_dim.13
  63.1 9.1 %all-to-all-start.3 = ((f16[8,32,256]{2,1,0:T(8,128)(2,1)}), f16[8,32,256]{2,1,0:T(8,128)(2,1)S(1)}, u32[]{:S(2)}, u32[]{:S(2)}) async-start(f16[8,32,256]{2,1,0:T(8,128)(2,1)} %broadcast_in_dim.13), calls=%async_computation.3 | async-start | bytes 262144 | tf_op jit(solution)/shard_map/all_to_all | solution.py:29
  72.2 0.1 broadcast_select_fusion.1
  72.3 3.3 %collective-permute-start.2 = (f16[768,128]{1,0:T(8,128)(2,1)S(1)}, f16[768,128]{1,0:T(8,128)(2,1)S(1)}, u32[]{:S(2)}, u32[]{:S(2)}) collective-permute-start(f16[768,128]{1,0:T(8,128)(2,1)S(1)} %get-tuple-element.42), channel_id=1, source_target_pairs={{1,2},{3,4},{5,6},{7,8},{9,10},{11,12},{13,14},{15,16},{17,18},{19... | collective-permute-start | bytes 589832 | tf_op jit(solution)/shard_map/ppermute | solution.py:38
  75.6 1.5 %all-to-all-done.3 = f16[8,32,256]{2,1,0:T(8,128)(2,1)S(1)} async-done(((f16[8,32,256]{2,1,0:T(8,128)(2,1)}), f16[8,32,256]{2,1,0:T(8,128)(2,1)S(1)}, u32[]{:S(2)}, u32[]{:S(2)}) %all-to-all-start.3) | async-done | bytes 131104 | tf_op jit(solution)/shard_map/all_to_all | solution.py:29
  77.2 0.7 broadcast_in_dim.14
  77.9 6.3 %all-to-all-start.4 = ((f16[8,32,256]{2,1,0:T(8,128)(2,1)}), f16[8,32,256]{2,1,0:T(8,128)(2,1)S(1)}, u32[]{:S(2)}, u32[]{:S(2)}) async-start(f16[8,32,256]{2,1,0:T(8,128)(2,1)} %broadcast_in_dim.14), calls=%async_computation.4 | async-start | bytes 262144 | tf_op jit(solution)/shard_map/all_to_all | solution.py:29
  84.1 0.6 convert_bitcast_fusion
  84.8 2.3 %collective-permute-start.3 = (f16[768,128]{1,0:T(8,128)(2,1)S(1)}, f16[768,128]{1,0:T(8,128)(2,1)S(1)}, u32[]{:S(2)}, u32[]{:S(2)}) collective-permute-start(f16[768,128]{1,0:T(8,128)(2,1)S(1)} %get-tuple-element.40), channel_id=1, source_target_pairs={{0,1},{1,0},{2,3},{3,2},{4,5},{5,4},{6,7},{7,6},{8,9},{9,8},{10,11... | collective-permute-start | bytes 589832 | tf_op jit(solution)/shard_map/ppermute | solution.py:33
  87.1 0.7 all-to-all-done.4
  87.8 0.7 fusion
  88.5 0.0 collective-permute-done.2
  88.5 0.0 collective-permute-done.3
  88.5 0.8 add_convert_fusion
  (10 shorter events, 0.1 us)
Async XLA Ops:
  0.6 10.2 %copy-start = (bf16[768,256]{1,0:T(8,128)(2,1)S(1)}, bf16[768,256]{1,0:T(8,128)(2,1)}, u32[]{:S(2)}) copy-start(bf16[768,256]{1,0:T(8,128)(2,1)} %param.11) | copy-start | bytes 1179652
  0.6 13.1 %collective-permute-start = (bf16[768,128]{1,0:T(8,128)(2,1)}, bf16[768,128]{1,0:T(8,128)(2,1)S(1)}, u32[]{:S(2)}, u32[]{:S(2)}) collective-permute-start(bf16[768,128]{1,0:T(8,128)(2,1)} %x_ref.3), channel_id=1, source_target_pairs={{1,2},{3,4},{5,6},{7,8},{9,10},{11,12},{13,14},{15,16},{17,18},{19... | collective-permute-start | bytes 589832 | tf_op jit(solution)/shard_map/ppermute | solution.py:38
  5.3 8.4 %collective-permute-start.1 = (bf16[768,128]{1,0:T(8,128)(2,1)}, bf16[768,128]{1,0:T(8,128)(2,1)S(1)}, u32[]{:S(2)}, u32[]{:S(2)}) collective-permute-start(bf16[768,128]{1,0:T(8,128)(2,1)} %x_ref.3), channel_id=1, source_target_pairs={{0,1},{1,0},{2,3},{3,2},{4,5},{5,4},{6,7},{7,6},{8,9},{9,8},{10,11... | collective-permute-start | bytes 589832 | tf_op jit(solution)/shard_map/ppermute | solution.py:33
  10.3 0.8 copy-start.7
  10.3 0.9 %copy-start.4 = (bf16[768,128]{1,0:T(8,128)(2,1)S(1)}, bf16[768,128]{1,0:T(8,128)(2,1)}, u32[]{:S(2)}) copy-start(bf16[768,128]{1,0:T(8,128)(2,1)} %x_ref.3) | copy-start | bytes 589828
  10.3 0.9 %copy-start.5 = (bf16[128,256]{1,0:T(8,128)(2,1)S(1)}, bf16[128,256]{1,0:T(8,128)(2,1)}, u32[]{:S(2)}) copy-start(bf16[128,256]{1,0:T(8,128)(2,1)} %ws_ref.1) | copy-start | bytes 196612
  10.3 1.0 %copy-start.6 = (bf16[128,256]{1,0:T(8,128)(2,1)S(1)}, bf16[128,256]{1,0:T(8,128)(2,1)}, u32[]{:S(2)}) copy-start(bf16[128,256]{1,0:T(8,128)(2,1)} %wn_ref.1) | copy-start | bytes 196612
  11.2 2.0 %copy-start.1 = (bf16[768,2304]{1,0:T(8,128)(2,1)S(1)}, bf16[768,2304]{1,0:T(8,128)(2,1)}, u32[]{:S(2)}) copy-start(bf16[768,2304]{1,0:T(8,128)(2,1)} %adj_ref.5) | copy-start | bytes 10616836
  13.2 2.0 %copy-start.2 = (bf16[768,2304]{1,0:T(8,128)(2,1)S(1)}, bf16[768,2304]{1,0:T(8,128)(2,1)}, u32[]{:S(2)}) copy-start(bf16[768,2304]{1,0:T(8,128)(2,1)} %adj_ref.5) | copy-start | bytes 10616836
  49.9 12.5 %all-to-all-start.2 = ((f16[8,32,256]{2,1,0:T(8,128)(2,1)}), f16[8,32,256]{2,1,0:T(8,128)(2,1)S(1)}, u32[]{:S(2)}, u32[]{:S(2)}) async-start(f16[8,32,256]{2,1,0:T(8,128)(2,1)} %bitcast.5), calls=%async_computation.2 | async-start | bytes 262144 | tf_op jit(solution)/shard_map/all_to_all | solution.py:29
  59.2 2.0 %copy-start.3 = (bf16[768,2304]{1,0:T(8,128)(2,1)S(1)}, bf16[768,2304]{1,0:T(8,128)(2,1)}, u32[]{:S(2)}) copy-start(bf16[768,2304]{1,0:T(8,128)(2,1)} %adj_ref.5) | copy-start | bytes 10616836
  63.1 14.0 %all-to-all-start.3 = ((f16[8,32,256]{2,1,0:T(8,128)(2,1)}), f16[8,32,256]{2,1,0:T(8,128)(2,1)S(1)}, u32[]{:S(2)}, u32[]{:S(2)}) async-start(f16[8,32,256]{2,1,0:T(8,128)(2,1)} %broadcast_in_dim.13), calls=%async_computation.3 | async-start | bytes 262144 | tf_op jit(solution)/shard_map/all_to_all | solution.py:29
  72.3 16.2 %collective-permute-start.2 = (f16[768,128]{1,0:T(8,128)(2,1)S(1)}, f16[768,128]{1,0:T(8,128)(2,1)S(1)}, u32[]{:S(2)}, u32[]{:S(2)}) collective-permute-start(f16[768,128]{1,0:T(8,128)(2,1)S(1)} %get-tuple-element.42), channel_id=1, source_target_pairs={{1,2},{3,4},{5,6},{7,8},{9,10},{11,12},{13,14},{15,16},{17,18},{19... | collective-permute-start | bytes 589832 | tf_op jit(solution)/shard_map/ppermute | solution.py:38
  77.9 9.9 %all-to-all-start.4 = ((f16[8,32,256]{2,1,0:T(8,128)(2,1)}), f16[8,32,256]{2,1,0:T(8,128)(2,1)S(1)}, u32[]{:S(2)}, u32[]{:S(2)}) async-start(f16[8,32,256]{2,1,0:T(8,128)(2,1)} %broadcast_in_dim.14), calls=%async_computation.4 | async-start | bytes 262144 | tf_op jit(solution)/shard_map/all_to_all | solution.py:29
  84.8 3.8 %collective-permute-start.3 = (f16[768,128]{1,0:T(8,128)(2,1)S(1)}, f16[768,128]{1,0:T(8,128)(2,1)S(1)}, u32[]{:S(2)}, u32[]{:S(2)}) collective-permute-start(f16[768,128]{1,0:T(8,128)(2,1)S(1)} %get-tuple-element.40), channel_id=1, source_target_pairs={{0,1},{1,0},{2,3},{3,2},{4,5},{5,4},{6,7},{7,6},{8,9},{9,8},{10,11... | collective-permute-start | bytes 589832 | tf_op jit(solution)/shard_map/ppermute | solution.py:33

commit v3 on v2

--- a/solution.py
+++ b/solution.py
@@ -42,30 +42,33 @@
     side_ref[0] = even_ref[0]
 
 
-def own_kernel(adj_ref, x_ref, ws_ref, wn_ref, own_ref, w_ref, wt_ref):
+def wide(block):
+    return jnp.concatenate([block, jnp.ones_like(block)], axis=1)
+
+
+def near_kernel(even_ref, adj_ref, near_ref, x_ref, part_ref, far_ref, sem):
     rows = x_ref.shape[0]
-    x = x_ref[...]
-    wide = jnp.concatenate([x, jnp.ones_like(x)], axis=1)
-    own_ref[...] = mm(adj_ref[:, rows : 2 * rows], wide)
-    w = jnp.concatenate([ws_ref[...], wn_ref[...]], axis=0)
-    w_ref[...] = w
-    wt_ref[...] = w.T
-
-
-def agg_kernel(even_ref, adj_ref, far_ref, near_ref, own_ref, x_ref, wt_ref, both_ref, deg_ref, part_ref):
-    rows, feats = x_ref.shape
-    even = even_ref[0] == 1
-    far, near = far_ref[...], near_ref[...]
-    ones = jnp.ones_like(far)
-    before = jnp.concatenate([jnp.where(even, far, near), ones], axis=1)
-    after = jnp.concatenate([jnp.where(even, near, far), ones], axis=1)
-    total = own_ref[...] + mm(adj_ref[:, :rows], before) + mm(adj_ref[:, 2 * rows :], after)
+    even = even_ref[0]
+    at = pl.multiple_of((1 - even) * 2 * rows, rows)
+    copy = pltpu.make_async_copy(adj_ref.at[:, pl.ds(at, rows)], far_ref, sem)
+    copy.start()
+    at = pl.multiple_of(even * rows, rows)
+    near, x = near_ref[...], x_ref[...]
+    pair = jnp.concatenate([jnp.where(even == 1, x, near), jnp.where(even == 1, near, x)], axis=0)
+    part_ref[...] = mm(adj_ref[:, pl.ds(at, 2 * rows)], wide(pair))
+    copy.wait()
+
+
+def agg_kernel(adj_ref, far_ref, sum_ref, x_ref, ws_ref, wn_ref, both_ref, deg_ref, part_ref):
+    feats = x_ref.shape[1]
+    total = sum_ref[...] + mm(adj_ref[...], wide(far_ref[...]))
     deg = 1.0 + total[:, feats:]
-    deg_ref[...] = deg
     agg = (total[:, :feats] / deg).astype(BF16)
     both = jnp.concatenate([x_ref[...], agg], axis=1).T
     both_ref[...] = both
-    part_ref[...] = mm(wt_ref[...], both) * 128.0
+    weights = jnp.concatenate([ws_ref[...], wn_ref[...]], axis=0).T
+    part_ref[...] = mm(weights, both) * 128.0
+    deg_ref[...] = deg
 
 
 def act_kernel(pre_ref, bias_ref, up_ref, hidden_ref, dpre_ref):
@@ -86,13 +89,20 @@
     grad_ref[...] = contract(both_ref[...], gathered(dpre_ref), 1, 1)
 
 
-def back_kernel(adj_ref, deg_ref, w_ref, dpre_ref, first_ref, mid_ref, last_ref):
+def back_kernel(adj_ref, deg_ref, ws_ref, wn_ref, dpre_ref, first_ref, mid_ref, last_ref):
     rows, feats = mid_ref.shape
     dpre = gathered(dpre_ref)
-    scaled = (mm(w_ref[feats:], dpre) / deg_ref[...]).astype(BF16)
+    scaled = (mm(wn_ref[...], dpre) / deg_ref[...].T).astype(BF16)
     first_ref[...] = mm(scaled, adj_ref[:, :rows]).T
     last_ref[...] = mm(scaled, adj_ref[:, 2 * rows :]).T
-    mid_ref[...] = (mm(scaled, adj_ref[:, rows : 2 * rows]) + mm(w_ref[:feats], dpre)).T
+    mid_ref[...] = (mm(scaled, adj_ref[:, rows : 2 * rows]) + mm(ws_ref[...], dpre)).T
+
+
+def finish_kernel(grad_ref, mid_ref, halo_ref, total_ref, self_ref, neigh_ref):
+    feats = self_ref.shape[0]
+    total_ref[...] = (mid_ref[...] + halo_ref[...]).astype(BF16)
+    self_ref[...] = grad_ref[:feats]
+    neigh_ref[...] = grad_ref[feats:]
 
 
 def cost(us):
@@ -116,28 +126,28 @@
         out_shape=shape((1,), jnp.int32),
         cost_estimate=cost(5),
     )(even.astype(jnp.int32).reshape(1))
-    own, w_both, w_flip = pl.pallas_call(
-        own_kernel,
-        in_specs=[VMEM] * 4,
-        out_specs=[VMEM] * 3,
-        out_shape=[shape((rows, 2 * feats), F32), shape((2 * feats, hid), BF16), shape((hid, 2 * feats), BF16)],
-        compiler_params=PARAMS,
-        cost_estimate=cost(3),
-    )(adjacency, features, w_self, w_neigh)
+    summed, adj_far = pl.pallas_call(
+        near_kernel,
+        in_specs=[SMEM] + [VMEM] * 3,
+        out_specs=[VMEM] * 2,
+        out_shape=[shape((rows, 2 * feats), F32), shape((rows, rows), BF16)],
+        scratch_shapes=[pltpu.SemaphoreType.DMA(())],
+        compiler_params=PARAMS,
+        cost_estimate=cost(2),
+    )(side, adjacency, near, features)
     both, deg, part = pl.pallas_call(
         agg_kernel,
-        in_specs=[SMEM] + [VMEM] * 6,
+        in_specs=[VMEM] * 6,
         out_specs=[VMEM] * 3,
         out_shape=[shape((2 * feats, rows), BF16), shape((rows, feats), F32), shape((hid, rows), F32)],
         compiler_params=PARAMS,
         cost_estimate=cost(3),
-    )(side, adjacency, far, near, own, features, w_flip)
+    )(adj_far, far, summed, features, w_self, w_neigh)
     offset = lax.axis_index("z") * width
     bias_part = jnp.broadcast_to(lax.dynamic_slice_in_dim(bias, offset, width)[:, None], (width, 128))
     upstream = lax.dynamic_slice_in_dim(cotangent, offset, width, 1).T
-    deg = deg[:, 0][None]
     sent = part.astype(F16).reshape(feat, width, rows)
-    sent, deg, upstream, bias_part = lax.optimization_barrier((sent, deg, upstream, bias_part))
+    sent, upstream, bias_part = lax.optimization_barrier((sent, upstream, bias_part))
     got = jnp.sum(exchange(sent, "z").astype(F32), axis=0)
     hidden, dpre = pl.pallas_call(
         act_kernel,
@@ -166,12 +176,12 @@
 
     first, mid, last = pl.pallas_call(
         back_kernel,
-        in_specs=[VMEM] * 4,
+        in_specs=[VMEM] * 5,
         out_specs=[VMEM] * 3,
         out_shape=[shape((rows, feats), F32)] * 3,
         compiler_params=PARAMS,
         cost_estimate=pl.CostEstimate(flops=6 * rows * rows * feats, bytes_accessed=6 * rows * rows, transcendentals=0),
-    )(adjacency, deg, w_both, dpre)
+    )(adjacency, deg, w_self, w_neigh, dpre)
     first = (first * 0.125).astype(F16)
     last = (last * 0.125).astype(F16)
     from_far = swap_chips(jnp.where(even, first, last))
@@ -180,8 +190,13 @@
     piece = jnp.broadcast_to((jnp.sum(piece.astype(F32), axis=0) * 0.125).astype(F16), (X * C, share, hid))
     from_near = swap_cores(near)
     grad = exchange_down(piece, ("x", "c")).reshape(2 * feats, hid).astype(F32) * 32.0
-    total = mid + 8.0 * (from_far.astype(F32) + from_near.astype(F32))
-    return hidden.astype(BF16).T, total.astype(BF16), grad[:feats], grad[feats:]
+    halo = 8.0 * (from_far.astype(F32) + from_near.astype(F32))
+    total, grad_self, grad_neigh = pl.pallas_call(
+        finish_kernel,
+        out_shape=[shape((rows, feats), BF16), shape((feats, hid), F32), shape((feats, hid), F32)],
+        compiler_params=PARAMS,
+    )(grad, mid, halo)
+    return hidden.astype(BF16).T, total, grad_self, grad_neigh
 
 
 def solution(mesh):

time: 90 us -> 89.1 us (0.990)
  local copies, waits for them, and re-layouts: 8.21 us -> 5.82 us
  blocking collectives: 31.4 us -> 32.5 us
  Pallas kernels: 4.12 us -> 5.05 us
    ppermute x2, starting transfers between devices: 7.28 us -> 11.2 us  [swap_cores(): return lax.ppermute(block, 'c', [(0, 1), (1, 0)])]
    all_to_all x1, blocking collectives: 11.1 us -> 14.4 us  [exchange_down(): lax.all_to_all(blocks, axes, 0, 0, tiled=True, axis_index_groups=[list(ra...]
    ppermute x2, starting transfers between devices: 7.92 us -> 5.39 us  [swap_chips(): return lax.ppermute(block, VERT, pairs + [(j, i) for i, j in pairs])]
    all_to_all x3, starting transfers between devices: 24.7 us -> 22.5 us  [exchange_down(): lax.all_to_all(blocks, axes, 0, 0, tiled=True, axis_index_groups=[list(ra...]
    all_to_all x1, blocking collectives: 20.3 us -> 18.2 us  [exchange(): return lax.all_to_all(blocks, axes, 0, 0, tiled=True)]
    unnamed x17 -> x15, local copies, waits for them, and re-layouts: 5.7 us -> 4.21 us
    pallas_call x3 -> x4, Pallas kernels: 3.19 us -> 4.12 us  [the longest x1 1.55 us: body(): pl.pallas_call(near_kernel, in_specs=[SMEM] + [VMEM] * 3, out_specs=[VMEM...]
  transfers between devices with their start and end apart: 7 -> 7, of which waited for: 3 -> 5; matrix products, arithmetic and copies ran while one was open for 3% -> 2% of each run, Pallas kernels for 2% -> 3%
where the time goes in v3:
time: 89.1 us; the launch traced here: 88.4 us
  starting transfers between devices  39.1 us (44%)
  blocking collectives  32.5 us (36%)
  local copies, waits for them, and re-layouts  5.82 us (7%)
  Pallas kernels  5.05 us (6%)
  waiting for transfers between devices  3.38 us (4%)
  other arithmetic  1.64 us (2%)
    all_to_all x3, starting transfers between devices, exchange_down(): lax.all_to_all(blocks, axes, 0, 0, tiled=True, axis_index_groups=[list(ra...  22.5 us
    all_to_all x1, blocking collectives, exchange(): return lax.all_to_all(blocks, axes, 0, 0, tiled=True)  18.2 us
    all_to_all x1, blocking collectives, exchange_down(): lax.all_to_all(blocks, axes, 0, 0, tiled=True, axis_index_groups=[list(ra...  14.4 us
    ppermute x2, starting transfers between devices, swap_cores(): return lax.ppermute(block, 'c', [(0, 1), (1, 0)])  11.2 us
    ppermute x2, starting transfers between devices, swap_chips(): return lax.ppermute(block, VERT, pairs + [(j, i) for i, j in pairs])  5.39 us
    unnamed x15, local copies, waits for them, and re-layouts  4.21 us
    all_to_all x3, waiting for transfers between devices, exchange_down(): lax.all_to_all(blocks, axes, 0, 0, tiled=True, axis_index_groups=[list(ra...  1.93 us
  transfers between devices with their start and end apart: 7, of which 5 were waited for; matrix products, arithmetic and copies ran while one was open for 2% of the time, Pallas kernels for 3%

profile of v3, /device:TPU:1, one launch (start us, length us, event | category | flops | bytes accessed | tf_op | source)
XLA Modules:
  0.0 88.4 jit_solution(13943527038627140760)
XLA Ops:
  0.6 0.0 copy-start
  0.6 8.9 %collective-permute-start = (bf16[768,128]{1,0:T(8,128)(2,1)}, bf16[768,128]{1,0:T(8,128)(2,1)S(1)}, u32[]{:S(2)}, u32[]{:S(2)}) collective-permute-start(bf16[768,128]{1,0:T(8,128)(2,1)} %x_ref.3), channel_id=1, source_target_pairs={{0,1},{1,0},{2,3},{3,2},{4,5},{5,4},{6,7},{7,6},{8,9},{9,8},{10,11... | collective-permute-start | bytes 589832 | tf_op jit(solution)/shard_map/ppermute | solution.py:33
  9.6 1.9 %collective-permute-start.1 = (bf16[768,128]{1,0:T(8,128)(2,1)}, bf16[768,128]{1,0:T(8,128)(2,1)S(1)}, u32[]{:S(2)}, u32[]{:S(2)}) collective-permute-start(bf16[768,128]{1,0:T(8,128)(2,1)} %x_ref.3), channel_id=1, source_target_pairs={{1,2},{3,4},{5,6},{7,8},{9,10},{11,12},{13,14},{15,16},{17,18},{19... | collective-permute-start | bytes 589832 | tf_op jit(solution)/shard_map/ppermute | solution.py:38
  11.5 0.0 copy-start.6
  11.5 0.0 copy-start.5
  11.5 0.5 shard_map.93.even_ref
  12.1 0.0 copy-done
  12.1 0.1 constant_dynamic-slice_fusion
  12.2 0.1 copy.12
  12.3 0.0 copy-done.6
  12.3 0.1 dynamic_slice.7
  12.4 0.0 collective-permute-done.near_ref
  12.4 0.1 copy-done.5
  12.5 0.0 copy-start.1
  12.5 2.0 %copy-done.1 = bf16[768,2304]{1,0:T(8,128)(2,1)S(1)} copy-done((bf16[768,2304]{1,0:T(8,128)(2,1)S(1)}, bf16[768,2304]{1,0:T(8,128)(2,1)}, u32[]{:S(2)}) %copy-start.1) | copy-done | bytes 3538968
  14.5 0.0 copy-start.3
  14.5 0.0 copy-start.4
  14.5 1.5 %shard_map.94 = (f32[768,256]{1,0:T(8,128)S(1)}, bf16[768,768]{1,0:T(8,128)(2,1)S(1)}) custom-call(s32[1]{0:T(128)} %shard_map.93.even_ref, bf16[768,2304]{1,0:T(8,128)(2,1)S(1)} %copy-done.1, bf16[768,128]{1,0:T(8,128)(2,1)S(1)} %collective-permute-done.near_ref, bf16[768,128]{1,0:T(8,128)(2,1)S(1)} %copy-done.5), custom_call_target="tpu_custom_call" | custom-call | flops 2000000000 | tf_op jit(solution)/shard_map/pallas_call | solution.py:129
  16.0 0.7 collective-permute-done.1.far_ref
  16.8 0.0 copy-done.3
  16.8 0.0 copy-done.4
  16.8 0.8 shard_map.95
  17.6 0.1 broadcast_in_dim.12.bias_ref
  17.7 18.2 %all_to_all.25 = f16[8,32,768]{2,1,0:T(8,128)(2,1)S(1)} all-to-all(f16[8,32,768]{2,1,0:T(8,128)(2,1)S(1)} %bitcast.12), channel_id=1, replica_groups=mesh['z'=8,'y'=8,'x'=4,'c'=2] {'z'}, dimensions={0} | all-to-all | bytes 786432 | tf_op jit(solution)/shard_map/all_to_all | solution.py:25
  35.9 0.1 convert_reduce_fusion.pre_ref
  35.9 0.1 shard_map.96
  36.1 14.4 %all_to_all.26 = bf16[8,32,768]{2,1,0:T(8,128)(2,1)S(1)} all-to-all(bf16[8,32,768]{2,1,0:T(8,128)(2,1)S(1)} %get-tuple-element.30), channel_id=1, replica_groups={{448,384,320,256,192,128,64,0},{449,385,321,257,193,129,65,1},{450,386,..., dimensions={0} | all-to-all | bytes 786432 | tf_op jit(solution)/shard_map/all_to_all | solution.py:29
  50.4 0.3 shard_map.97
  50.7 0.7 convert_element_type.44
  51.4 8.6 %all-to-all-start.2 = ((f16[8,32,256]{2,1,0:T(8,128)(2,1)}), f16[8,32,256]{2,1,0:T(8,128)(2,1)S(1)}, u32[]{:S(2)}, u32[]{:S(2)}) async-start(f16[8,32,256]{2,1,0:T(8,128)(2,1)} %bitcast.5), calls=%async_computation.2 | async-start | bytes 262144 | tf_op jit(solution)/shard_map/all_to_all | solution.py:29
  60.1 0.0 copy-start.2
  60.1 2.0 %copy-done.2 = bf16[768,2304]{1,0:T(8,128)(2,1)S(1)} copy-done((bf16[768,2304]{1,0:T(8,128)(2,1)S(1)}, bf16[768,2304]{1,0:T(8,128)(2,1)}, u32[]{:S(2)}) %copy-start.2) | copy-done | bytes 3538968
  62.1 0.9 %shard_map.98 = (f32[768,128]{1,0:T(8,128)S(1)}, f32[768,128]{1,0:T(8,128)S(1)}, f32[768,128]{1,0:T(8,128)S(1)}) custom-call(bf16[768,2304]{1,0:T(8,128)(2,1)S(1)} %copy-done.2, f32[768,128]{1,0:T(8,128)S(1)} %get-tuple-element.35.deg_ref, bf16[128,256]{1,0:T(8,128)(2,1)S(1)} %copy-done.3, bf16[128,256]{1,0:T(8,128)(2,1)S(1)} %copy-done.4, ...), custom_call_target="tpu_custom_call" | custom-call | flops 452984832 | bytes 3538944 | tf_op jit(solution)/shard_map/pallas_call | solution.py:177
  63.0 0.3 all-to-all-done.2
  63.3 0.7 broadcast_in_dim.13
  64.0 7.1 %all-to-all-start.3 = ((f16[8,32,256]{2,1,0:T(8,128)(2,1)}), f16[8,32,256]{2,1,0:T(8,128)(2,1)S(1)}, u32[]{:S(2)}, u32[]{:S(2)}) async-start(f16[8,32,256]{2,1,0:T(8,128)(2,1)} %broadcast_in_dim.13), calls=%async_computation.3 | async-start | bytes 262144 | tf_op jit(solution)/shard_map/all_to_all | solution.py:29
  71.1 0.1 broadcast_select_fusion
  71.2 3.5 %collective-permute-start.2 = (f16[768,128]{1,0:T(8,128)(2,1)S(1)}, f16[768,128]{1,0:T(8,128)(2,1)S(1)}, u32[]{:S(2)}, u32[]{:S(2)}) collective-permute-start(f16[768,128]{1,0:T(8,128)(2,1)S(1)} %get-tuple-element.44), channel_id=1, source_target_pairs={{1,2},{3,4},{5,6},{7,8},{9,10},{11,12},{13,14},{15,16},{17,18},{19... | collective-permute-start | bytes 589832 | tf_op jit(solution)/shard_map/ppermute | solution.py:38
  74.7 1.3 %all-to-all-done.3 = f16[8,32,256]{2,1,0:T(8,128)(2,1)S(1)} async-done(((f16[8,32,256]{2,1,0:T(8,128)(2,1)}), f16[8,32,256]{2,1,0:T(8,128)(2,1)S(1)}, u32[]{:S(2)}, u32[]{:S(2)}) %all-to-all-start.3) | async-done | bytes 131104 | tf_op jit(solution)/shard_map/all_to_all | solution.py:29
  76.1 0.7 broadcast_in_dim.14
  76.8 6.8 %all-to-all-start.4 = ((f16[8,32,256]{2,1,0:T(8,128)(2,1)}), f16[8,32,256]{2,1,0:T(8,128)(2,1)S(1)}, u32[]{:S(2)}, u32[]{:S(2)}) async-start(f16[8,32,256]{2,1,0:T(8,128)(2,1)} %broadcast_in_dim.14), calls=%async_computation.4 | async-start | bytes 262144 | tf_op jit(solution)/shard_map/all_to_all | solution.py:29
  83.5 0.6 convert_bitcast_fusion
  84.1 2.3 %collective-permute-start.3 = (f16[768,128]{1,0:T(8,128)(2,1)S(1)}, f16[768,128]{1,0:T(8,128)(2,1)S(1)}, u32[]{:S(2)}, u32[]{:S(2)}) collective-permute-start(f16[768,128]{1,0:T(8,128)(2,1)S(1)} %get-tuple-element.40), channel_id=1, source_target_pairs={{0,1},{1,0},{2,3},{3,2},{4,5},{5,4},{6,7},{7,6},{8,9},{9,8},{10,11... | collective-permute-start | bytes 589832 | tf_op jit(solution)/shard_map/ppermute | solution.py:33
  86.5 0.3 all-to-all-done.4
  86.8 0.0 collective-permute-done.2
  86.8 0.7 collective-permute-done.3
  87.5 0.1 add_multiply_fusion.halo_ref
  87.6 0.8 shard_map.99
  (6 shorter events, 0.1 us)
Async XLA Ops:
  0.6 11.4 %copy-start = (bf16[768,256]{1,0:T(8,128)(2,1)S(1)}, bf16[768,256]{1,0:T(8,128)(2,1)}, u32[]{:S(2)}) copy-start(bf16[768,256]{1,0:T(8,128)(2,1)} %param.11) | copy-start | bytes 1179652
  0.6 11.8 %collective-permute-start = (bf16[768,128]{1,0:T(8,128)(2,1)}, bf16[768,128]{1,0:T(8,128)(2,1)S(1)}, u32[]{:S(2)}, u32[]{:S(2)}) collective-permute-start(bf16[768,128]{1,0:T(8,128)(2,1)} %x_ref.3), channel_id=1, source_target_pairs={{0,1},{1,0},{2,3},{3,2},{4,5},{5,4},{6,7},{7,6},{8,9},{9,8},{10,11... | collective-permute-start | bytes 589832 | tf_op jit(solution)/shard_map/ppermute | solution.py:33
  9.6 7.2 %collective-permute-start.1 = (bf16[768,128]{1,0:T(8,128)(2,1)}, bf16[768,128]{1,0:T(8,128)(2,1)S(1)}, u32[]{:S(2)}, u32[]{:S(2)}) collective-permute-start(bf16[768,128]{1,0:T(8,128)(2,1)} %x_ref.3), channel_id=1, source_target_pairs={{1,2},{3,4},{5,6},{7,8},{9,10},{11,12},{13,14},{15,16},{17,18},{19... | collective-permute-start | bytes 589832 | tf_op jit(solution)/shard_map/ppermute | solution.py:38
  11.5 0.8 copy-start.6
  11.5 1.0 %copy-start.5 = (bf16[768,128]{1,0:T(8,128)(2,1)S(1)}, bf16[768,128]{1,0:T(8,128)(2,1)}, u32[]{:S(2)}) copy-start(bf16[768,128]{1,0:T(8,128)(2,1)} %x_ref.3) | copy-start | bytes 589828
  12.5 2.0 %copy-start.1 = (bf16[768,2304]{1,0:T(8,128)(2,1)S(1)}, bf16[768,2304]{1,0:T(8,128)(2,1)}, u32[]{:S(2)}) copy-start(bf16[768,2304]{1,0:T(8,128)(2,1)} %adj_ref.3) | copy-start | bytes 10616836
  14.5 2.3 %copy-start.3 = (bf16[128,256]{1,0:T(8,128)(2,1)S(1)}, bf16[128,256]{1,0:T(8,128)(2,1)}, u32[]{:S(2)}) copy-start(bf16[128,256]{1,0:T(8,128)(2,1)} %ws_ref.3) | copy-start | bytes 196612
  14.5 2.3 %copy-start.4 = (bf16[128,256]{1,0:T(8,128)(2,1)S(1)}, bf16[128,256]{1,0:T(8,128)(2,1)}, u32[]{:S(2)}) copy-start(bf16[128,256]{1,0:T(8,128)(2,1)} %wn_ref.3) | copy-start | bytes 196612
  51.4 11.9 %all-to-all-start.2 = ((f16[8,32,256]{2,1,0:T(8,128)(2,1)}), f16[8,32,256]{2,1,0:T(8,128)(2,1)S(1)}, u32[]{:S(2)}, u32[]{:S(2)}) async-start(f16[8,32,256]{2,1,0:T(8,128)(2,1)} %bitcast.5), calls=%async_computation.2 | async-start | bytes 262144 | tf_op jit(solution)/shard_map/all_to_all | solution.py:29
  60.1 2.0 %copy-start.2 = (bf16[768,2304]{1,0:T(8,128)(2,1)S(1)}, bf16[768,2304]{1,0:T(8,128)(2,1)}, u32[]{:S(2)}) copy-start(bf16[768,2304]{1,0:T(8,128)(2,1)} %adj_ref.3) | copy-start | bytes 10616836
  64.0 12.0 %all-to-all-start.3 = ((f16[8,32,256]{2,1,0:T(8,128)(2,1)}), f16[8,32,256]{2,1,0:T(8,128)(2,1)S(1)}, u32[]{:S(2)}, u32[]{:S(2)}) async-start(f16[8,32,256]{2,1,0:T(8,128)(2,1)} %broadcast_in_dim.13), calls=%async_computation.3 | async-start | bytes 262144 | tf_op jit(solution)/shard_map/all_to_all | solution.py:29
  71.2 15.6 %collective-permute-start.2 = (f16[768,128]{1,0:T(8,128)(2,1)S(1)}, f16[768,128]{1,0:T(8,128)(2,1)S(1)}, u32[]{:S(2)}, u32[]{:S(2)}) collective-permute-start(f16[768,128]{1,0:T(8,128)(2,1)S(1)} %get-tuple-element.44), channel_id=1, source_target_pairs={{1,2},{3,4},{5,6},{7,8},{9,10},{11,12},{13,14},{15,16},{17,18},{19... | collective-permute-start | bytes 589832 | tf_op jit(solution)/shard_map/ppermute | solution.py:38
  76.8 10.0 %all-to-all-start.4 = ((f16[8,32,256]{2,1,0:T(8,128)(2,1)}), f16[8,32,256]{2,1,0:T(8,128)(2,1)S(1)}, u32[]{:S(2)}, u32[]{:S(2)}) async-start(f16[8,32,256]{2,1,0:T(8,128)(2,1)} %broadcast_in_dim.14), calls=%async_computation.4 | async-start | bytes 262144 | tf_op jit(solution)/shard_map/all_to_all | solution.py:29
  84.1 3.4 %collective-permute-start.3 = (f16[768,128]{1,0:T(8,128)(2,1)S(1)}, f16[768,128]{1,0:T(8,128)(2,1)S(1)}, u32[]{:S(2)}, u32[]{:S(2)}) collective-permute-start(f16[768,128]{1,0:T(8,128)(2,1)S(1)} %get-tuple-element.40), channel_id=1, source_target_pairs={{0,1},{1,0},{2,3},{3,2},{4,5},{5,4},{6,7},{7,6},{8,9},{9,8},{10,11... | collective-permute-start | bytes 589832 | tf_op jit(solution)/shard_map/ppermute | solution.py:33

commit v4 on v3

v4 whole, which is shorter than its diff:
```python
import jax
import jax.numpy as jnp
from jax import lax
from jax.experimental import pallas as pl
from jax.experimental.pallas import tpu as pltpu
from jax.sharding import Mesh, PartitionSpec as P

F32, BF16, F16 = jnp.float32, jnp.bfloat16, jnp.float16
Y, X, C = 8, 4, 2
VERT = ("y", "x", "c")
PARAMS = pltpu.CompilerParams(vmem_limit_bytes=16 * 1024 * 1024)
VMEM = pl.BlockSpec()


def contract(a, b, da, db):
    return lax.dot_general(a, b, (((da,), (db,)), ((), ())), preferred_element_type=F32)


def mm(a, b):
    return jnp.dot(a, b, preferred_element_type=F32)


def exchange(blocks, axes):
    return lax.all_to_all(blocks, axes, 0, 0, tiled=True)


def exchange_down(blocks, axes):
    return lax.all_to_all(blocks, axes, 0, 0, tiled=True, axis_index_groups=[list(range(7, -1, -1))])


def swap_cores(block):
    return lax.ppermute(block, "c", [(0, 1), (1, 0)])


def swap_chips(block):
    pairs = [(i, i + 1) for i in range(1, Y * X * C - 1, 2)]
    return lax.ppermute(block, VERT, pairs + [(j, i) for i, j in pairs])


def ones_kernel(ones_ref):
    ones_ref[...] = jnp.ones_like(ones_ref)


def slabs(adj_ref, first, count):
    rows = adj_ref.shape[0]
    return adj_ref[:, pl.ds(pl.multiple_of(first * rows, rows), count * rows)]


def far_kernel(adj_ref, far_ref, x_ref, ones_ref, cot_ref, sum_ref, up_ref, flipped):
    core, width = lax.axis_index("c"), up_ref.shape[0]
    far, x, ones = far_ref[...], x_ref[...], ones_ref[...]
    pair = jnp.concatenate([jnp.where(core == 0, far, x), jnp.where(core == 0, x, far)], axis=0)
    wide = jnp.concatenate([pair, jnp.concatenate([ones, ones], axis=0)], axis=1)
    sum_ref[...] = mm(slabs(adj_ref, core, 2), wide)
    flipped[...] = cot_ref[...].T
    up_ref[...] = flipped[pl.ds(pl.multiple_of(lax.axis_index("z") * width, width), width)]


def agg_kernel(adj_ref, near_ref, ones_ref, sum_ref, x_ref, ws_ref, wn_ref, bias_ref, both_ref, deg_ref, part_ref, column_ref, columns):
    feats = x_ref.shape[1]
    wide = jnp.concatenate([near_ref[...], ones_ref[...]], axis=1)
    total = sum_ref[...] + mm(slabs(adj_ref, 2 - 2 * lax.axis_index("c"), 1), wide)
    deg = 1.0 + total[:, feats:]
    agg = (total[:, :feats] / deg).astype(BF16)
    deg_ref[...] = deg.T[: deg_ref.shape[0]]
    both = jnp.concatenate([x_ref[...], agg], axis=1).T
    both_ref[...] = both
    weights = jnp.concatenate([ws_ref[...], wn_ref[...]], axis=0).T
    part_ref[...] = mm(weights, both) * 128.0
    width = column_ref.shape[0]
    columns[...] = jnp.broadcast_to(bias_ref[...], (columns.shape[1], columns.shape[0])).T
    column_ref[...] = columns[pl.ds(pl.multiple_of(lax.axis_index("z") * width, width), width)]


def act_kernel(pre_ref, bias_ref, up_ref, hidden_ref, dpre_ref):
    pre = pre_ref[...] * (1.0 / 128.0) + bias_ref[:, :1]
    sig = jax.nn.sigmoid(pre)
    hidden_ref[...] = pre * sig
    dpre = (up_ref[...].astype(F32) * sig * (1.0 + pre * (1.0 - sig))).astype(BF16)
    for i in range(dpre_ref.shape[0]):
        dpre_ref[i] = dpre


def gathered(ref):
    size = ref.shape[0] // 8
    return jnp.concatenate([ref[i * size : (i + 1) * size] for i in range(7, -1, -1)], axis=0)


def grad_kernel(both_ref, dpre_ref, grad_ref):
    grad_ref[...] = contract(both_ref[...], gathered(dpre_ref), 1, 1)


def back_kernel(adj_ref, deg_ref, ws_ref, wn_ref, dpre_ref, far_ref, near_ref, mid_ref):
    core = lax.axis_index("c")
    dpre = gathered(dpre_ref)
    scaled = (mm(wn_ref[...], dpre) / deg_ref[:1]).astype(BF16)

    def back(slab):
        return mm(scaled, slabs(adj_ref, slab, 1))

    far_ref[...] = back(2 * core).T
    near_ref[...] = back(2 - 2 * core).T
    mid_ref[...] = (back(1) + mm(ws_ref[...], dpre)).T


def finish_kernel(grad_ref, mid_ref, halo_ref, total_ref, self_ref, neigh_ref):
    feats = self_ref.shape[0]
    total_ref[...] = (mid_ref[...] + halo_ref[...]).astype(BF16)
    self_ref[...] = grad_ref[:feats]
    neigh_ref[...] = grad_ref[feats:]


def cost(us):
    return pl.CostEstimate(flops=int(us * 1e9), bytes_accessed=0, transcendentals=0)


def body(features, adjacency, w_self, w_neigh, bias, cotangent):
    rows, feats = features.shape
    hid = bias.shape[0]
    feat = lax.axis_size("z")
    width = hid // feat
    shape = jax.ShapeDtypeStruct

    far = swap_chips(features)
    near = swap_cores(features)
    ones = pl.pallas_call(
        ones_kernel, out_shape=shape((rows, feats), BF16), compiler_params=PARAMS, cost_estimate=cost(5)
    )()
    summed, upstream = pl.pallas_call(
        far_kernel,
        out_shape=[shape((rows, 2 * feats), F32), shape((width, rows), BF16)],
        scratch_shapes=[pltpu.VMEM((hid, rows), BF16)],
        compiler_params=PARAMS,
        cost_estimate=cost(2),
    )(adjacency, far, features, ones, cotangent)
    both, deg, part, bias_part = pl.pallas_call(
        agg_kernel,
        out_shape=[shape((2 * feats, rows), BF16), shape((8, rows), F32), shape((hid, rows), F32), shape((width, 128), F32)],
        scratch_shapes=[pltpu.VMEM((hid, 128), F32)],
        compiler_params=PARAMS,
        cost_estimate=cost(3),
    )(adjacency, near, ones, summed, features, w_self, w_neigh, bias[None])
    sent = part.astype(F16).reshape(feat, width, rows)
    sent, upstream, bias_part = lax.optimization_barrier((sent, upstream, bias_part))
    got = jnp.sum(exchange(sent, "z").astype(F32), axis=0)
    hidden, dpre = pl.pallas_call(
        act_kernel,
        in_specs=[VMEM] * 3,
        out_specs=[VMEM] * 2,
        out_shape=[shape((width, rows), F32), shape((feat, width, rows), BF16)],
        compiler_params=PARAMS,
        cost_estimate=cost(1),
    )(got, bias_part, upstream)
    dpre, hidden = lax.optimization_barrier((exchange_down(dpre, "z"), hidden))
    dpre = dpre.reshape(hid, rows)

    grad = pl.pallas_call(
        grad_kernel,
        in_specs=[VMEM] * 2,
        out_specs=VMEM,
        out_shape=shape((2 * feats, hid), F32),
        compiler_params=PARAMS,
        cost_estimate=cost(1),
    )(both, dpre)
    share = 2 * feats // (X * C)
    far, near, mid = pl.pallas_call(
        back_kernel,
        in_specs=[VMEM] * 5,
        out_specs=[VMEM] * 3,
        out_shape=[shape((rows, feats), F32)] * 3,
        compiler_params=PARAMS,
        cost_estimate=pl.CostEstimate(flops=6 * rows * rows * feats, bytes_accessed=6 * rows * rows, transcendentals=0),
    )(adjacency, deg, w_self, w_neigh, dpre)
    piece = grad.astype(F16).reshape(X * C, share, hid)
    piece, far, near, mid = lax.optimization_barrier((piece, far, near, mid))
    piece = exchange_down(piece, ("x", "c"))
    piece = jnp.broadcast_to((jnp.sum(piece.astype(F32), axis=0) * 0.25).astype(F16), (Y, share, hid))

    from_far = swap_chips((far * 0.125).astype(F16))
    piece, near, hidden = lax.optimization_barrier((exchange_down(piece, "y"), near, hidden))
    piece = jnp.broadcast_to((jnp.sum(piece.astype(F32), axis=0) * 0.125).astype(F16), (X * C, share, hid))
    from_near = swap_cores((near * 0.125).astype(F16))
    grad = exchange_down(piece, ("x", "c")).reshape(2 * feats, hid).astype(F32) * 32.0
    halo = 8.0 * (from_far.astype(F32) + from_near.astype(F32))
    total, grad_self, grad_neigh = pl.pallas_call(
        finish_kernel,
        out_shape=[shape((rows, feats), BF16), shape((feats, hid), F32), shape((feats, hid), F32)],
        compiler_params=PARAMS,
    )(grad, mid, halo)
    return hidden.astype(BF16).T, total, grad_self, grad_neigh


def solution(mesh):
    split = Mesh(mesh.devices.reshape(-1, Y, X, C), ("z",) + VERT)
    rows = P(VERT, None)
    return jax.shard_map(
        body,
        mesh=split,
        in_specs=(P(VERT, "z"), rows, P("z", None), P("z", None), P(), rows),
        out_specs=(P(VERT, "z"), P(VERT, "z"), P("z", None), P("z", None)),
        check_vma=False,
    )
```

time: 89.1 us -> 85.6 us (0.961)
  blocking collectives: 32.5 us -> 46.5 us
  starting transfers between devices: 39.1 us -> 29.4 us
  local copies, waits for them, and re-layouts: 5.82 us -> 1.37 us
  Pallas kernels: 5.05 us -> 3.8 us
  waiting for transfers between devices: 3.38 us -> 2.16 us
    all_to_all x1 -> x2, blocking collectives: 14.4 us -> 23.3 us  [exchange_down(): lax.all_to_all(blocks, axes, 0, 0, tiled=True, axis_index_groups=[list(ra...]
    all_to_all x3 -> x2, starting transfers between devices: 22.5 us -> 13.9 us  [exchange_down(): lax.all_to_all(blocks, axes, 0, 0, tiled=True, axis_index_groups=[list(ra...]
    all_to_all x1, blocking collectives: 18.2 us -> 23.2 us  [exchange(): return lax.all_to_all(blocks, axes, 0, 0, tiled=True)]
    unnamed x15 -> x12, local copies, waits for them, and re-layouts: 4.21 us -> 0.03 us
    ppermute x2, starting transfers between devices: 11.2 us -> 7.29 us  [swap_cores(): return lax.ppermute(block, 'c', [(0, 1), (1, 0)])]
    ppermute x2, starting transfers between devices: 5.39 us -> 8.23 us  [swap_chips(): return lax.ppermute(block, VERT, pairs + [(j, i) for i, j in pairs])]
    pallas_call x3, Pallas kernels: 2.88 us -> 1.63 us  [the longest x1 0.81 us: body(): pl.pallas_call(agg_kernel, out_shape=[shape((2 * feats, rows), BF16), sha...]
    all_to_all x3 -> x2, waiting for transfers between devices: 1.93 us -> 1.66 us  [exchange_down(): lax.all_to_all(blocks, axes, 0, 0, tiled=True, axis_index_groups=[list(ra...]
  transfers between devices with their start and end apart: 7 -> 6, of which waited for: 5 -> 4; matrix products, arithmetic and copies ran while one was open for 2% -> 2% of each run, Pallas kernels for 3% -> 1%
where the time goes in v4:
time: 85.6 us; the launch traced here: 85.1 us
  blocking collectives  46.5 us (54%)
  starting transfers between devices  29.4 us (34%)
  Pallas kernels  3.8 us (4%)
  waiting for transfers between devices  2.16 us (3%)
  local copies, waits for them, and re-layouts  1.37 us (2%)
  other arithmetic  0.97 us (1%)
  between operations  0.86 us (1%)
    all_to_all x2, blocking collectives, exchange_down(): lax.all_to_all(blocks, axes, 0, 0, tiled=True, axis_index_groups=[list(ra...  23.3 us
    all_to_all x1, blocking collectives, exchange(): return lax.all_to_all(blocks, axes, 0, 0, tiled=True)  23.2 us
    all_to_all x2, starting transfers between devices, exchange_down(): lax.all_to_all(blocks, axes, 0, 0, tiled=True, axis_index_groups=[list(ra...  13.9 us
    ppermute x2, starting transfers between devices, swap_chips(): return lax.ppermute(block, VERT, pairs + [(j, i) for i, j in pairs])  8.23 us
    ppermute x2, starting transfers between devices, swap_cores(): return lax.ppermute(block, 'c', [(0, 1), (1, 0)])  7.29 us
  transfers between devices with their start and end apart: 6, of which 4 were waited for; matrix products, arithmetic and copies ran while one was open for 2% of the time, Pallas kernels for 1%

profile of v4, /device:TPU:1, one launch (start us, length us, event | category | flops | bytes accessed | tf_op | source)
XLA Modules:
  0.0 85.1 jit_solution(3986916972063006268)
XLA Ops:
  0.6 0.0 copy-start.4
  0.6 0.0 copy-start
  0.7 0.0 copy-start.3
  0.7 4.8 %collective-permute-start.1 = (bf16[768,128]{1,0:T(8,128)(2,1)}, bf16[768,128]{1,0:T(8,128)(2,1)S(1)}, u32[]{:S(2)}, u32[]{:S(2)}) collective-permute-start(bf16[768,128]{1,0:T(8,128)(2,1)} %x_ref.3), channel_id=1, source_target_pairs={{1,2},{3,4},{5,6},{7,8},{9,10},{11,12},{13,14},{15,16},{17,18},{19... | collective-permute-start | bytes 589832 | tf_op jit(solution)/shard_map/ppermute | solution.py:37
  5.4 5.0 %collective-permute-start = (bf16[768,128]{1,0:T(8,128)(2,1)}, bf16[768,128]{1,0:T(8,128)(2,1)S(1)}, u32[]{:S(2)}, u32[]{:S(2)}) collective-permute-start(bf16[768,128]{1,0:T(8,128)(2,1)} %x_ref.3), channel_id=1, source_target_pairs={{0,1},{1,0},{2,3},{3,2},{4,5},{5,4},{6,7},{7,6},{8,9},{9,8},{10,11... | collective-permute-start | bytes 589832 | tf_op jit(solution)/shard_map/ppermute | solution.py:32
  10.4 0.0 copy-start.1
  10.4 0.0 copy-start.2
  10.5 0.0 copy-start.5
  10.5 0.0 collective-permute-done.1.far_ref
  10.5 0.0 copy-done.4
  10.5 0.0 copy-done
  10.5 0.0 copy-done.3
  10.5 0.8 shard_map.94
  11.3 0.4 collective-permute-done.near_ref
  11.7 0.0 copy-done.1
  11.7 0.0 copy-done.2
  11.7 0.0 copy-done.5
  11.7 0.8 shard_map.95
  12.5 23.2 %all_to_all.25 = f16[8,32,768]{2,1,0:T(8,128)(2,1)S(1)} all-to-all(f16[8,32,768]{2,1,0:T(8,128)(2,1)S(1)} %bitcast.11), channel_id=1, replica_groups=mesh['z'=8,'y'=8,'x'=4,'c'=2] {'z'}, dimensions={0} | all-to-all | bytes 786432 | tf_op jit(solution)/shard_map/all_to_all | solution.py:24
  35.8 0.1 convert_reduce_fusion.pre_ref
  35.8 0.1 shard_map.96
  36.0 13.3 %all_to_all.26 = bf16[8,32,768]{2,1,0:T(8,128)(2,1)S(1)} all-to-all(bf16[8,32,768]{2,1,0:T(8,128)(2,1)S(1)} %get-tuple-element.38), channel_id=1, replica_groups={{448,384,320,256,192,128,64,0},{449,385,321,257,193,129,65,1},{450,386,..., dimensions={0} | all-to-all | bytes 786432 | tf_op jit(solution)/shard_map/all_to_all | solution.py:28
  49.3 0.3 shard_map.97
  49.6 0.9 %shard_map.98 = (f32[768,128]{1,0:T(8,128)S(1)}, f32[768,128]{1,0:T(8,128)S(1)}, f32[768,128]{1,0:T(8,128)S(1)}) custom-call(bf16[768,2304]{1,0:T(8,128)(2,1)S(1)} %copy-done, f32[8,768]{1,0:T(8,128)S(1)} %get-tuple-element.41.deg_ref, bf16[128,256]{1,0:T(8,128)(2,1)S(1)} %copy-done.1, bf16[128,256]{1,0:T(8,128)(2,1)S(1)} %copy-done.2, ...), custom_call_target="tpu_custom_call" | custom-call | flops 452984832 | bytes 3538944 | tf_op jit(solution)/shard_map/pallas_call | solution.py:166
  50.6 10.0 %all_to_all.27 = f16[8,32,256]{2,1,0:T(8,128)(2,1)S(1)} all-to-all(f16[8,32,256]{2,1,0:T(8,128)(2,1)S(1)} %bitcast.12), channel_id=1, replica_groups={{7,6,5,4,3,2,1,0},{15,14,13,12,11,10,9,8},{23,22,21,20,19,18,17,16},{31..., dimensions={0} | all-to-all | bytes 262144 | tf_op jit(solution)/shard_map/all_to_all | solution.py:28
  60.6 0.7 broadcast_in_dim.10
  61.2 7.1 %all-to-all-start.3 = ((f16[8,32,256]{2,1,0:T(8,128)(2,1)}), f16[8,32,256]{2,1,0:T(8,128)(2,1)S(1)}, u32[]{:S(2)}, u32[]{:S(2)}) async-start(f16[8,32,256]{2,1,0:T(8,128)(2,1)} %broadcast_in_dim.10), calls=%async_computation.3 | async-start | bytes 262144 | tf_op jit(solution)/shard_map/all_to_all | solution.py:28
  68.4 3.5 %collective-permute-start.2 = (f16[768,128]{1,0:T(8,128)(2,1)S(1)}, f16[768,128]{1,0:T(8,128)(2,1)S(1)}, u32[]{:S(2)}, u32[]{:S(2)}) collective-permute-start(f16[768,128]{1,0:T(8,128)(2,1)S(1)} %multiply_convert_fusion.1), channel_id=1, source_target_pairs={{1,2},{3,4},{5,6},{7,8},{9,10},{11,12},{13,14},{15,16},{17,18},{19... | collective-permute-start | bytes 589832 | tf_op jit(solution)/shard_map/ppermute | solution.py:37
  71.9 1.4 %all-to-all-done.3 = f16[8,32,256]{2,1,0:T(8,128)(2,1)S(1)} async-done(((f16[8,32,256]{2,1,0:T(8,128)(2,1)}), f16[8,32,256]{2,1,0:T(8,128)(2,1)S(1)}, u32[]{:S(2)}, u32[]{:S(2)}) %all-to-all-start.3) | async-done | bytes 131104 | tf_op jit(solution)/shard_map/all_to_all | solution.py:28
  73.3 0.7 broadcast_in_dim.11
  74.0 6.8 %all-to-all-start.4 = ((f16[8,32,256]{2,1,0:T(8,128)(2,1)}), f16[8,32,256]{2,1,0:T(8,128)(2,1)S(1)}, u32[]{:S(2)}, u32[]{:S(2)}) async-start(f16[8,32,256]{2,1,0:T(8,128)(2,1)} %broadcast_in_dim.11), calls=%async_computation.4 | async-start | bytes 262144 | tf_op jit(solution)/shard_map/all_to_all | solution.py:28
  80.8 2.3 %collective-permute-start.3 = (f16[768,128]{1,0:T(8,128)(2,1)S(1)}, f16[768,128]{1,0:T(8,128)(2,1)S(1)}, u32[]{:S(2)}, u32[]{:S(2)}) collective-permute-start(f16[768,128]{1,0:T(8,128)(2,1)S(1)} %multiply_convert_fusion), channel_id=1, source_target_pairs={{0,1},{1,0},{2,3},{3,2},{4,5},{5,4},{6,7},{7,6},{8,9},{9,8},{10,11... | collective-permute-start | bytes 589832 | tf_op jit(solution)/shard_map/ppermute | solution.py:32
  83.1 0.6 convert_bitcast_fusion
  83.8 0.2 all-to-all-done.4
  84.0 0.0 collective-permute-done.2
  84.1 0.1 collective-permute-done.3
  84.2 0.1 add_multiply_fusion.halo_ref
  84.2 0.8 shard_map.99
  (10 shorter events, 0.3 us)
Async XLA Ops:
  0.6 9.9 %copy-start.4 = (bf16[768,128]{1,0:T(8,128)(2,1)S(1)}, bf16[768,128]{1,0:T(8,128)(2,1)}, u32[]{:S(2)}) copy-start(bf16[768,128]{1,0:T(8,128)(2,1)} %x_ref.3) | copy-start | bytes 589828
  0.6 9.9 %copy-start = (bf16[768,2304]{1,0:T(8,128)(2,1)S(1)}, bf16[768,2304]{1,0:T(8,128)(2,1)}, u32[]{:S(2)}) copy-start(bf16[768,2304]{1,0:T(8,128)(2,1)} %adj_ref.5) | copy-start | bytes 10616836
  0.7 9.9 %copy-start.3 = (bf16[768,256]{1,0:T(8,128)(2,1)S(1)}, bf16[768,256]{1,0:T(8,128)(2,1)}, u32[]{:S(2)}) copy-start(bf16[768,256]{1,0:T(8,128)(2,1)} %cot_ref.1) | copy-start | bytes 1179652
  0.7 9.8 %collective-permute-start.1 = (bf16[768,128]{1,0:T(8,128)(2,1)}, bf16[768,128]{1,0:T(8,128)(2,1)S(1)}, u32[]{:S(2)}, u32[]{:S(2)}) collective-permute-start(bf16[768,128]{1,0:T(8,128)(2,1)} %x_ref.3), channel_id=1, source_target_pairs={{1,2},{3,4},{5,6},{7,8},{9,10},{11,12},{13,14},{15,16},{17,18},{19... | collective-permute-start | bytes 589832 | tf_op jit(solution)/shard_map/ppermute | solution.py:37
  5.4 6.2 %collective-permute-start = (bf16[768,128]{1,0:T(8,128)(2,1)}, bf16[768,128]{1,0:T(8,128)(2,1)S(1)}, u32[]{:S(2)}, u32[]{:S(2)}) collective-permute-start(bf16[768,128]{1,0:T(8,128)(2,1)} %x_ref.3), channel_id=1, source_target_pairs={{0,1},{1,0},{2,3},{3,2},{4,5},{5,4},{6,7},{7,6},{8,9},{9,8},{10,11... | collective-permute-start | bytes 589832 | tf_op jit(solution)/shard_map/ppermute | solution.py:32
  10.4 1.2 %copy-start.1 = (bf16[128,256]{1,0:T(8,128)(2,1)S(1)}, bf16[128,256]{1,0:T(8,128)(2,1)}, u32[]{:S(2)}) copy-start(bf16[128,256]{1,0:T(8,128)(2,1)} %ws_ref.3) | copy-start | bytes 196612
  10.4 1.2 %copy-start.2 = (bf16[128,256]{1,0:T(8,128)(2,1)S(1)}, bf16[128,256]{1,0:T(8,128)(2,1)}, u32[]{:S(2)}) copy-start(bf16[128,256]{1,0:T(8,128)(2,1)} %wn_ref.3) | copy-start | bytes 196612
  10.5 1.2 %copy-start.5 = (f32[256]{0:T(256)S(1)}, f32[256]{0:T(256)}, u32[]{:S(2)}) copy-start(f32[256]{0:T(256)} %param.10) | copy-start | bytes 3076
  61.2 12.0 %all-to-all-start.3 = ((f16[8,32,256]{2,1,0:T(8,128)(2,1)}), f16[8,32,256]{2,1,0:T(8,128)(2,1)S(1)}, u32[]{:S(2)}, u32[]{:S(2)}) async-start(f16[8,32,256]{2,1,0:T(8,128)(2,1)} %broadcast_in_dim.10), calls=%async_computation.3 | async-start | bytes 262144 | tf_op jit(solution)/shard_map/all_to_all | solution.py:28
  68.4 15.7 %collective-permute-start.2 = (f16[768,128]{1,0:T(8,128)(2,1)S(1)}, f16[768,128]{1,0:T(8,128)(2,1)S(1)}, u32[]{:S(2)}, u32[]{:S(2)}) collective-permute-start(f16[768,128]{1,0:T(8,128)(2,1)S(1)} %multiply_convert_fusion.1), channel_id=1, source_target_pairs={{1,2},{3,4},{5,6},{7,8},{9,10},{11,12},{13,14},{15,16},{17,18},{19... | collective-permute-start | bytes 589832 | tf_op jit(solution)/shard_map/ppermute | solution.py:37
  74.0 10.0 %all-to-all-start.4 = ((f16[8,32,256]{2,1,0:T(8,128)(2,1)}), f16[8,32,256]{2,1,0:T(8,128)(2,1)S(1)}, u32[]{:S(2)}, u32[]{:S(2)}) async-start(f16[8,32,256]{2,1,0:T(8,128)(2,1)} %broadcast_in_dim.11), calls=%async_computation.4 | async-start | bytes 262144 | tf_op jit(solution)/shard_map/all_to_all | solution.py:28
  80.8 3.4 %collective-permute-start.3 = (f16[768,128]{1,0:T(8,128)(2,1)S(1)}, f16[768,128]{1,0:T(8,128)(2,1)S(1)}, u32[]{:S(2)}, u32[]{:S(2)}) collective-permute-start(f16[768,128]{1,0:T(8,128)(2,1)S(1)} %multiply_convert_fusion), channel_id=1, source_target_pairs={{0,1},{1,0},{2,3},{3,2},{4,5},{5,4},{6,7},{7,6},{8,9},{9,8},{10,11... | collective-permute-start | bytes 589832 | tf_op jit(solution)/shard_map/ppermute | solution.py:32

commit v5 on v4

--- a/solution.py
+++ b/solution.py
@@ -46,17 +46,23 @@
     return adj_ref[:, pl.ds(pl.multiple_of(first * rows, rows), count * rows)]
 
 
-def far_kernel(adj_ref, far_ref, x_ref, ones_ref, cot_ref, sum_ref, up_ref, flipped):
-    core, width = lax.axis_index("c"), up_ref.shape[0]
-    far, x, ones = far_ref[...], x_ref[...], ones_ref[...]
-    pair = jnp.concatenate([jnp.where(core == 0, far, x), jnp.where(core == 0, x, far)], axis=0)
-    wide = jnp.concatenate([pair, jnp.concatenate([ones, ones], axis=0)], axis=1)
-    sum_ref[...] = mm(slabs(adj_ref, core, 2), wide)
-    flipped[...] = cot_ref[...].T
-    up_ref[...] = flipped[pl.ds(pl.multiple_of(lax.axis_index("z") * width, width), width)]
-
-
-def agg_kernel(adj_ref, near_ref, ones_ref, sum_ref, x_ref, ws_ref, wn_ref, bias_ref, both_ref, deg_ref, part_ref, column_ref, columns):
+def own_kernel(adj_ref, x_ref, ones_ref, cot_ref, ws_ref, wn_ref, bias_ref, sum_ref, up_ref, w_ref, column_ref, turned, columns):
+    width = up_ref.shape[0]
+    here = pl.ds(pl.multiple_of(lax.axis_index("z") * width, width), width)
+    sum_ref[...] = mm(slabs(adj_ref, 1, 1), jnp.concatenate([x_ref[...], ones_ref[...]], axis=1))
+    turned[...] = cot_ref[...].T
+    up_ref[...] = turned[here]
+    w_ref[...] = jnp.concatenate([ws_ref[...], wn_ref[...]], axis=0).T
+    columns[...] = jnp.broadcast_to(bias_ref[...], (columns.shape[1], columns.shape[0])).T
+    column_ref[...] = columns[here]
+
+
+def far_kernel(adj_ref, far_ref, ones_ref, own_ref, sum_ref):
+    wide = jnp.concatenate([far_ref[...], ones_ref[...]], axis=1)
+    sum_ref[...] = own_ref[...] + mm(slabs(adj_ref, 2 * lax.axis_index("c"), 1), wide)
+
+
+def agg_kernel(adj_ref, near_ref, ones_ref, sum_ref, x_ref, w_ref, both_ref, deg_ref, part_ref):
     feats = x_ref.shape[1]
     wide = jnp.concatenate([near_ref[...], ones_ref[...]], axis=1)
     total = sum_ref[...] + mm(slabs(adj_ref, 2 - 2 * lax.axis_index("c"), 1), wide)
@@ -65,11 +71,7 @@
     deg_ref[...] = deg.T[: deg_ref.shape[0]]
     both = jnp.concatenate([x_ref[...], agg], axis=1).T
     both_ref[...] = both
-    weights = jnp.concatenate([ws_ref[...], wn_ref[...]], axis=0).T
-    part_ref[...] = mm(weights, both) * 128.0
-    width = column_ref.shape[0]
-    columns[...] = jnp.broadcast_to(bias_ref[...], (columns.shape[1], columns.shape[0])).T
-    column_ref[...] = columns[pl.ds(pl.multiple_of(lax.axis_index("z") * width, width), width)]
+    part_ref[...] = mm(w_ref[...], both) * 128.0
 
 
 def act_kernel(pre_ref, bias_ref, up_ref, hidden_ref, dpre_ref):
@@ -126,20 +128,27 @@
     ones = pl.pallas_call(
         ones_kernel, out_shape=shape((rows, feats), BF16), compiler_params=PARAMS, cost_estimate=cost(5)
     )()
-    summed, upstream = pl.pallas_call(
-        far_kernel,
-        out_shape=[shape((rows, 2 * feats), F32), shape((width, rows), BF16)],
-        scratch_shapes=[pltpu.VMEM((hid, rows), BF16)],
+    own, upstream, weights, bias_part = pl.pallas_call(
+        own_kernel,
+        out_shape=[
+            shape((rows, 2 * feats), F32),
+            shape((width, rows), BF16),
+            shape((hid, 2 * feats), BF16),
+            shape((width, 128), F32),
+        ],
+        scratch_shapes=[pltpu.VMEM((hid, rows), BF16), pltpu.VMEM((hid, 128), F32)],
         compiler_params=PARAMS,
         cost_estimate=cost(2),
-    )(adjacency, far, features, ones, cotangent)
-    both, deg, part, bias_part = pl.pallas_call(
+    )(adjacency, features, ones, cotangent, w_self, w_neigh, bias[None])
+    summed = pl.pallas_call(
+        far_kernel, out_shape=shape((rows, 2 * feats), F32), compiler_params=PARAMS, cost_estimate=cost(2)
+    )(adjacency, far, ones, own)
+    both, deg, part = pl.pallas_call(
         agg_kernel,
-        out_shape=[shape((2 * feats, rows), BF16), shape((8, rows), F32), shape((hid, rows), F32), shape((width, 128), F32)],
-        scratch_shapes=[pltpu.VMEM((hid, 128), F32)],
+        out_shape=[shape((2 * feats, rows), BF16), shape((8, rows), F32), shape((hid, rows), F32)],
         compiler_params=PARAMS,
         cost_estimate=cost(3),
-    )(adjacency, near, ones, summed, features, w_self, w_neigh, bias[None])
+    )(adjacency, near, ones, summed, features, weights)
     sent = part.astype(F16).reshape(feat, width, rows)
     sent, upstream, bias_part = lax.optimization_barrier((sent, upstream, bias_part))
     got = jnp.sum(exchange(sent, "z").astype(F32), axis=0)

time: 85.6 us -> 85.7 us (level)
  no operation moved by 1% of the time
where the time goes in v5:
time: 85.7 us; the launch traced here: 85.1 us
  blocking collectives  46.2 us (54%)
  starting transfers between devices  29.7 us (35%)
  Pallas kernels  4 us (5%)
  waiting for transfers between devices  1.96 us (2%)
  local copies, waits for them, and re-layouts  1.36 us (2%)
  other arithmetic  0.97 us (1%)
  between operations  0.89 us (1%)
    all_to_all x2, blocking collectives, exchange_down(): lax.all_to_all(blocks, axes, 0, 0, tiled=True, axis_index_groups=[list(ra...  23.3 us
    all_to_all x1, blocking collectives, exchange(): return lax.all_to_all(blocks, axes, 0, 0, tiled=True)  22.9 us
    all_to_all x2, starting transfers between devices, exchange_down(): lax.all_to_all(blocks, axes, 0, 0, tiled=True, axis_index_groups=[list(ra...  14.2 us
    ppermute x2, starting transfers between devices, swap_chips(): return lax.ppermute(block, VERT, pairs + [(j, i) for i, j in pairs])  8.24 us
    ppermute x2, starting transfers between devices, swap_cores(): return lax.ppermute(block, 'c', [(0, 1), (1, 0)])  7.29 us
  transfers between devices with their start and end apart: 6, of which 4 were waited for; matrix products, arithmetic and copies ran while one was open for 2% of the time, Pallas kernels for 1%

profile of v5, /device:TPU:1, one launch (start us, length us, event | category | flops | bytes accessed | tf_op | source)
XLA Modules:
  0.0 85.1 jit_solution(6184599680785016857)
XLA Ops:
  0.6 0.0 copy-start.4
  0.6 0.0 copy-start
  0.7 0.0 copy-start.2
  0.7 0.0 copy-start.1
  0.7 0.0 copy-start.3
  0.7 0.0 copy-start.5
  0.7 4.8 %collective-permute-start.1 = (bf16[768,128]{1,0:T(8,128)(2,1)}, bf16[768,128]{1,0:T(8,128)(2,1)S(1)}, u32[]{:S(2)}, u32[]{:S(2)}) collective-permute-start(bf16[768,128]{1,0:T(8,128)(2,1)} %x_ref.3), channel_id=1, source_target_pairs={{1,2},{3,4},{5,6},{7,8},{9,10},{11,12},{13,14},{15,16},{17,18},{19... | collective-permute-start | bytes 589832 | tf_op jit(solution)/shard_map/ppermute | solution.py:37
  5.5 5.0 %collective-permute-start = (bf16[768,128]{1,0:T(8,128)(2,1)}, bf16[768,128]{1,0:T(8,128)(2,1)S(1)}, u32[]{:S(2)}, u32[]{:S(2)}) collective-permute-start(bf16[768,128]{1,0:T(8,128)(2,1)} %x_ref.3), channel_id=1, source_target_pairs={{0,1},{1,0},{2,3},{3,2},{4,5},{5,4},{6,7},{7,6},{8,9},{9,8},{10,11... | collective-permute-start | bytes 589832 | tf_op jit(solution)/shard_map/ppermute | solution.py:32
  10.5 0.0 copy-done.4
  10.5 0.0 copy-done
  10.5 0.0 copy-done.2
  10.5 0.0 copy-done.1
  10.5 0.0 copy-done.3
  10.5 0.0 copy-done.5
  10.5 0.5 shard_map.94
  11.0 0.0 collective-permute-done.1.far_ref
  11.0 0.5 shard_map.95.sum_ref
  11.5 0.2 collective-permute-done.near_ref
  11.7 0.8 shard_map.96
  12.6 22.9 %all_to_all.25 = f16[8,32,768]{2,1,0:T(8,128)(2,1)S(1)} all-to-all(f16[8,32,768]{2,1,0:T(8,128)(2,1)S(1)} %bitcast.11), channel_id=1, replica_groups=mesh['z'=8,'y'=8,'x'=4,'c'=2] {'z'}, dimensions={0} | all-to-all | bytes 786432 | tf_op jit(solution)/shard_map/all_to_all | solution.py:24
  35.4 0.1 convert_reduce_fusion.pre_ref
  35.5 0.1 shard_map.97
  35.6 13.2 %all_to_all.26 = bf16[8,32,768]{2,1,0:T(8,128)(2,1)S(1)} all-to-all(bf16[8,32,768]{2,1,0:T(8,128)(2,1)S(1)} %get-tuple-element.40), channel_id=1, replica_groups={{448,384,320,256,192,128,64,0},{449,385,321,257,193,129,65,1},{450,386,..., dimensions={0} | all-to-all | bytes 786432 | tf_op jit(solution)/shard_map/all_to_all | solution.py:28
  48.8 0.3 shard_map.98
  49.1 1.0 %shard_map.99 = (f32[768,128]{1,0:T(8,128)S(1)}, f32[768,128]{1,0:T(8,128)S(1)}, f32[768,128]{1,0:T(8,128)S(1)}) custom-call(bf16[768,2304]{1,0:T(8,128)(2,1)S(1)} %copy-done, f32[8,768]{1,0:T(8,128)S(1)} %get-tuple-element.43.deg_ref, bf16[128,256]{1,0:T(8,128)(2,1)S(1)} %copy-done.1, bf16[128,256]{1,0:T(8,128)(2,1)S(1)} %copy-done.2, ...), custom_call_target="tpu_custom_call" | custom-call | flops 452984832 | bytes 3538944 | tf_op jit(solution)/shard_map/pallas_call | solution.py:175
  50.1 10.1 %all_to_all.27 = f16[8,32,256]{2,1,0:T(8,128)(2,1)S(1)} all-to-all(f16[8,32,256]{2,1,0:T(8,128)(2,1)S(1)} %bitcast.12), channel_id=1, replica_groups={{7,6,5,4,3,2,1,0},{15,14,13,12,11,10,9,8},{23,22,21,20,19,18,17,16},{31..., dimensions={0} | all-to-all | bytes 262144 | tf_op jit(solution)/shard_map/all_to_all | solution.py:28
  60.3 0.7 broadcast_in_dim.10
  60.9 7.4 %all-to-all-start.3 = ((f16[8,32,256]{2,1,0:T(8,128)(2,1)}), f16[8,32,256]{2,1,0:T(8,128)(2,1)S(1)}, u32[]{:S(2)}, u32[]{:S(2)}) async-start(f16[8,32,256]{2,1,0:T(8,128)(2,1)} %broadcast_in_dim.10), calls=%async_computation.3 | async-start | bytes 262144 | tf_op jit(solution)/shard_map/all_to_all | solution.py:28
  68.4 3.5 %collective-permute-start.2 = (f16[768,128]{1,0:T(8,128)(2,1)S(1)}, f16[768,128]{1,0:T(8,128)(2,1)S(1)}, u32[]{:S(2)}, u32[]{:S(2)}) collective-permute-start(f16[768,128]{1,0:T(8,128)(2,1)S(1)} %multiply_convert_fusion.1), channel_id=1, source_target_pairs={{1,2},{3,4},{5,6},{7,8},{9,10},{11,12},{13,14},{15,16},{17,18},{19... | collective-permute-start | bytes 589832 | tf_op jit(solution)/shard_map/ppermute | solution.py:37
  71.9 1.4 %all-to-all-done.3 = f16[8,32,256]{2,1,0:T(8,128)(2,1)S(1)} async-done(((f16[8,32,256]{2,1,0:T(8,128)(2,1)}), f16[8,32,256]{2,1,0:T(8,128)(2,1)S(1)}, u32[]{:S(2)}, u32[]{:S(2)}) %all-to-all-start.3) | async-done | bytes 131104 | tf_op jit(solution)/shard_map/all_to_all | solution.py:28
  73.4 0.7 broadcast_in_dim.11
  74.0 6.8 %all-to-all-start.4 = ((f16[8,32,256]{2,1,0:T(8,128)(2,1)}), f16[8,32,256]{2,1,0:T(8,128)(2,1)S(1)}, u32[]{:S(2)}, u32[]{:S(2)}) async-start(f16[8,32,256]{2,1,0:T(8,128)(2,1)} %broadcast_in_dim.11), calls=%async_computation.4 | async-start | bytes 262144 | tf_op jit(solution)/shard_map/all_to_all | solution.py:28
  80.8 2.3 %collective-permute-start.3 = (f16[768,128]{1,0:T(8,128)(2,1)S(1)}, f16[768,128]{1,0:T(8,128)(2,1)S(1)}, u32[]{:S(2)}, u32[]{:S(2)}) collective-permute-start(f16[768,128]{1,0:T(8,128)(2,1)S(1)} %multiply_convert_fusion), channel_id=1, source_target_pairs={{0,1},{1,0},{2,3},{3,2},{4,5},{5,4},{6,7},{7,6},{8,9},{9,8},{10,11... | collective-permute-start | bytes 589832 | tf_op jit(solution)/shard_map/ppermute | solution.py:32
  83.2 0.6 convert_bitcast_fusion
  83.8 0.2 all-to-all-done.4
  84.1 0.0 collective-permute-done.2
  84.1 0.1 collective-permute-done.3
  84.2 0.1 add_multiply_fusion.halo_ref
  84.3 0.8 shard_map.100
  (10 shorter events, 0.3 us)
Async XLA Ops:
  0.6 9.8 %copy-start.4 = (bf16[768,128]{1,0:T(8,128)(2,1)S(1)}, bf16[768,128]{1,0:T(8,128)(2,1)}, u32[]{:S(2)}) copy-start(bf16[768,128]{1,0:T(8,128)(2,1)} %x_ref.3) | copy-start | bytes 589828
  0.6 9.8 %copy-start = (bf16[768,2304]{1,0:T(8,128)(2,1)S(1)}, bf16[768,2304]{1,0:T(8,128)(2,1)}, u32[]{:S(2)}) copy-start(bf16[768,2304]{1,0:T(8,128)(2,1)} %adj_ref.7) | copy-start | bytes 10616836
  0.7 9.8 %copy-start.2 = (bf16[128,256]{1,0:T(8,128)(2,1)S(1)}, bf16[128,256]{1,0:T(8,128)(2,1)}, u32[]{:S(2)}) copy-start(bf16[128,256]{1,0:T(8,128)(2,1)} %wn_ref.3) | copy-start | bytes 196612
  0.7 9.8 %copy-start.1 = (bf16[128,256]{1,0:T(8,128)(2,1)S(1)}, bf16[128,256]{1,0:T(8,128)(2,1)}, u32[]{:S(2)}) copy-start(bf16[128,256]{1,0:T(8,128)(2,1)} %ws_ref.3) | copy-start | bytes 196612
  0.7 9.8 %copy-start.3 = (bf16[768,256]{1,0:T(8,128)(2,1)S(1)}, bf16[768,256]{1,0:T(8,128)(2,1)}, u32[]{:S(2)}) copy-start(bf16[768,256]{1,0:T(8,128)(2,1)} %cot_ref.1) | copy-start | bytes 1179652
  0.7 9.8 %copy-start.5 = (f32[256]{0:T(256)S(1)}, f32[256]{0:T(256)}, u32[]{:S(2)}) copy-start(f32[256]{0:T(256)} %param.10) | copy-start | bytes 3076
  0.7 10.3 %collective-permute-start.1 = (bf16[768,128]{1,0:T(8,128)(2,1)}, bf16[768,128]{1,0:T(8,128)(2,1)S(1)}, u32[]{:S(2)}, u32[]{:S(2)}) collective-permute-start(bf16[768,128]{1,0:T(8,128)(2,1)} %x_ref.3), channel_id=1, source_target_pairs={{1,2},{3,4},{5,6},{7,8},{9,10},{11,12},{13,14},{15,16},{17,18},{19... | collective-permute-start | bytes 589832 | tf_op jit(solution)/shard_map/ppermute | solution.py:37
  5.5 6.2 %collective-permute-start = (bf16[768,128]{1,0:T(8,128)(2,1)}, bf16[768,128]{1,0:T(8,128)(2,1)S(1)}, u32[]{:S(2)}, u32[]{:S(2)}) collective-permute-start(bf16[768,128]{1,0:T(8,128)(2,1)} %x_ref.3), channel_id=1, source_target_pairs={{0,1},{1,0},{2,3},{3,2},{4,5},{5,4},{6,7},{7,6},{8,9},{9,8},{10,11... | collective-permute-start | bytes 589832 | tf_op jit(solution)/shard_map/ppermute | solution.py:32
  60.9 12.4 %all-to-all-start.3 = ((f16[8,32,256]{2,1,0:T(8,128)(2,1)}), f16[8,32,256]{2,1,0:T(8,128)(2,1)S(1)}, u32[]{:S(2)}, u32[]{:S(2)}) async-start(f16[8,32,256]{2,1,0:T(8,128)(2,1)} %broadcast_in_dim.10), calls=%async_computation.3 | async-start | bytes 262144 | tf_op jit(solution)/shard_map/all_to_all | solution.py:28
  68.4 15.7 %collective-permute-start.2 = (f16[768,128]{1,0:T(8,128)(2,1)S(1)}, f16[768,128]{1,0:T(8,128)(2,1)S(1)}, u32[]{:S(2)}, u32[]{:S(2)}) collective-permute-start(f16[768,128]{1,0:T(8,128)(2,1)S(1)} %multiply_convert_fusion.1), channel_id=1, source_target_pairs={{1,2},{3,4},{5,6},{7,8},{9,10},{11,12},{13,14},{15,16},{17,18},{19... | collective-permute-start | bytes 589832 | tf_op jit(solution)/shard_map/ppermute | solution.py:37
  74.0 10.0 %all-to-all-start.4 = ((f16[8,32,256]{2,1,0:T(8,128)(2,1)}), f16[8,32,256]{2,1,0:T(8,128)(2,1)S(1)}, u32[]{:S(2)}, u32[]{:S(2)}) async-start(f16[8,32,256]{2,1,0:T(8,128)(2,1)} %broadcast_in_dim.11), calls=%async_computation.4 | async-start | bytes 262144 | tf_op jit(solution)/shard_map/all_to_all | solution.py:28
  80.8 3.4 %collective-permute-start.3 = (f16[768,128]{1,0:T(8,128)(2,1)S(1)}, f16[768,128]{1,0:T(8,128)(2,1)S(1)}, u32[]{:S(2)}, u32[]{:S(2)}) collective-permute-start(f16[768,128]{1,0:T(8,128)(2,1)S(1)} %multiply_convert_fusion), channel_id=1, source_target_pairs={{0,1},{1,0},{2,3},{3,2},{4,5},{5,4},{6,7},{7,6},{8,9},{9,8},{10,11... | collective-permute-start | bytes 589832 | tf_op jit(solution)/shard_map/ppermute | solution.py:32

commit v6 on v5

--- a/solution.py
+++ b/solution.py
@@ -26,6 +26,10 @@
 
 def exchange_down(blocks, axes):
     return lax.all_to_all(blocks, axes, 0, 0, tiled=True, axis_index_groups=[list(range(7, -1, -1))])
+
+
+def exchange_rows(blocks):
+    return lax.all_to_all(blocks, "y", 0, 0, tiled=True, axis_index_groups=[[4, 5, 3, 6, 2, 7, 1, 0]])
 
 
 def swap_cores(block):
@@ -186,7 +190,7 @@
     piece = jnp.broadcast_to((jnp.sum(piece.astype(F32), axis=0) * 0.25).astype(F16), (Y, share, hid))
 
     from_far = swap_chips((far * 0.125).astype(F16))
-    piece, near, hidden = lax.optimization_barrier((exchange_down(piece, "y"), near, hidden))
+    piece, near, hidden = lax.optimization_barrier((exchange_rows(piece), near, hidden))
     piece = jnp.broadcast_to((jnp.sum(piece.astype(F32), axis=0) * 0.125).astype(F16), (X * C, share, hid))
     from_near = swap_cores((near * 0.125).astype(F16))
     grad = exchange_down(piece, ("x", "c")).reshape(2 * feats, hid).astype(F32) * 32.0

time: 85.7 us -> 85 us (level)
  waiting for transfers between devices: 1.96 us -> 0.55 us
    all_to_all x0 -> x1, starting transfers between devices: none -> 8.85 us  [exchange_rows(): lax.all_to_all(blocks, 'y', 0, 0, tiled=True, axis_index_groups=[[4, 5, 3...]
    all_to_all x2 -> x1, starting transfers between devices: 14.2 us -> 6.36 us  [exchange_down(): lax.all_to_all(blocks, axes, 0, 0, tiled=True, axis_index_groups=[list(ra...]
    all_to_all x2 -> x1, waiting for transfers between devices: 1.65 us -> 0.23 us  [exchange_down(): lax.all_to_all(blocks, axes, 0, 0, tiled=True, axis_index_groups=[list(ra...]
  transfers between devices with their start and end apart: 6 -> 6, of which waited for: 4 -> 3; matrix products, arithmetic and copies ran while one was open for 2% -> 2% of each run, Pallas kernels for 1% -> 1%
where the time goes in v6:
time: 85 us; the launch traced here: 84.4 us
  blocking collectives  46.2 us (54%)
  starting transfers between devices  30.5 us (36%)
  Pallas kernels  4 us (5%)
  local copies, waits for them, and re-layouts  1.36 us (2%)
  other arithmetic  0.97 us (1%)
  between operations  0.9 us (1%)
    all_to_all x2, blocking collectives, exchange_down(): lax.all_to_all(blocks, axes, 0, 0, tiled=True, axis_index_groups=[list(ra...  23.3 us
    all_to_all x1, blocking collectives, exchange(): return lax.all_to_all(blocks, axes, 0, 0, tiled=True)  22.9 us
    all_to_all x1, starting transfers between devices, exchange_rows(): lax.all_to_all(blocks, 'y', 0, 0, tiled=True, axis_index_groups=[[4, 5, 3...  8.85 us
    ppermute x2, starting transfers between devices, swap_chips(): return lax.ppermute(block, VERT, pairs + [(j, i) for i, j in pairs])  7.96 us
    ppermute x2, starting transfers between devices, swap_cores(): return lax.ppermute(block, 'c', [(0, 1), (1, 0)])  7.29 us
    all_to_all x1, starting transfers between devices, exchange_down(): lax.all_to_all(blocks, axes, 0, 0, tiled=True, axis_index_groups=[list(ra...  6.36 us
  transfers between devices with their start and end apart: 6, of which 3 were waited for; matrix products, arithmetic and copies ran while one was open for 2% of the time, Pallas kernels for 1%

profile of v6, /device:TPU:1, one launch (start us, length us, event | category | flops | bytes accessed | tf_op | source)
XLA Modules:
  0.0 84.4 jit_solution(14828778881391267856)
XLA Ops:
  0.6 0.0 copy-start.4
  0.6 0.0 copy-start
  0.7 0.0 copy-start.2
  0.7 0.0 copy-start.1
  0.7 0.0 copy-start.3
  0.7 0.0 copy-start.5
  0.7 4.8 %collective-permute-start.1 = (bf16[768,128]{1,0:T(8,128)(2,1)}, bf16[768,128]{1,0:T(8,128)(2,1)S(1)}, u32[]{:S(2)}, u32[]{:S(2)}) collective-permute-start(bf16[768,128]{1,0:T(8,128)(2,1)} %x_ref.3), channel_id=1, source_target_pairs={{1,2},{3,4},{5,6},{7,8},{9,10},{11,12},{13,14},{15,16},{17,18},{19... | collective-permute-start | bytes 589832 | tf_op jit(solution)/shard_map/ppermute | solution.py:41
  5.5 5.0 %collective-permute-start = (bf16[768,128]{1,0:T(8,128)(2,1)}, bf16[768,128]{1,0:T(8,128)(2,1)S(1)}, u32[]{:S(2)}, u32[]{:S(2)}) collective-permute-start(bf16[768,128]{1,0:T(8,128)(2,1)} %x_ref.3), channel_id=1, source_target_pairs={{0,1},{1,0},{2,3},{3,2},{4,5},{5,4},{6,7},{7,6},{8,9},{9,8},{10,11... | collective-permute-start | bytes 589832 | tf_op jit(solution)/shard_map/ppermute | solution.py:36
  10.5 0.0 copy-done.4
  10.5 0.0 copy-done
  10.5 0.0 copy-done.2
  10.5 0.0 copy-done.1
  10.5 0.0 copy-done.3
  10.5 0.0 copy-done.5
  10.5 0.5 shard_map.94
  11.0 0.0 collective-permute-done.1.far_ref
  11.0 0.5 shard_map.95.sum_ref
  11.5 0.2 collective-permute-done.near_ref
  11.7 0.8 shard_map.96
  12.6 22.9 %all_to_all.25 = f16[8,32,768]{2,1,0:T(8,128)(2,1)S(1)} all-to-all(f16[8,32,768]{2,1,0:T(8,128)(2,1)S(1)} %bitcast.11), channel_id=1, replica_groups=mesh['z'=8,'y'=8,'x'=4,'c'=2] {'z'}, dimensions={0} | all-to-all | bytes 786432 | tf_op jit(solution)/shard_map/all_to_all | solution.py:24
  35.4 0.1 convert_reduce_fusion.pre_ref
  35.5 0.1 shard_map.97
  35.6 13.2 %all_to_all.26 = bf16[8,32,768]{2,1,0:T(8,128)(2,1)S(1)} all-to-all(bf16[8,32,768]{2,1,0:T(8,128)(2,1)S(1)} %get-tuple-element.40), channel_id=1, replica_groups={{448,384,320,256,192,128,64,0},{449,385,321,257,193,129,65,1},{450,386,..., dimensions={0} | all-to-all | bytes 786432 | tf_op jit(solution)/shard_map/all_to_all | solution.py:28
  48.8 0.3 shard_map.98
  49.1 1.0 %shard_map.99 = (f32[768,128]{1,0:T(8,128)S(1)}, f32[768,128]{1,0:T(8,128)S(1)}, f32[768,128]{1,0:T(8,128)S(1)}) custom-call(bf16[768,2304]{1,0:T(8,128)(2,1)S(1)} %copy-done, f32[8,768]{1,0:T(8,128)S(1)} %get-tuple-element.43.deg_ref, bf16[128,256]{1,0:T(8,128)(2,1)S(1)} %copy-done.1, bf16[128,256]{1,0:T(8,128)(2,1)S(1)} %copy-done.2, ...), custom_call_target="tpu_custom_call" | custom-call | flops 452984832 | bytes 3538944 | tf_op jit(solution)/shard_map/pallas_call | solution.py:179
  50.1 10.1 %all_to_all.27 = f16[8,32,256]{2,1,0:T(8,128)(2,1)S(1)} all-to-all(f16[8,32,256]{2,1,0:T(8,128)(2,1)S(1)} %bitcast.12), channel_id=1, replica_groups={{7,6,5,4,3,2,1,0},{15,14,13,12,11,10,9,8},{23,22,21,20,19,18,17,16},{31..., dimensions={0} | all-to-all | bytes 262144 | tf_op jit(solution)/shard_map/all_to_all | solution.py:28
  60.3 0.7 broadcast_in_dim.10
  60.9 8.9 %all-to-all-start.3 = ((f16[8,32,256]{2,1,0:T(8,128)(2,1)}), f16[8,32,256]{2,1,0:T(8,128)(2,1)S(1)}, u32[]{:S(2)}, u32[]{:S(2)}) async-start(f16[8,32,256]{2,1,0:T(8,128)(2,1)} %broadcast_in_dim.10), calls=%async_computation.3 | async-start | bytes 262144 | tf_op jit(solution)/shard_map/all_to_all | solution.py:32
  69.8 3.2 %collective-permute-start.2 = (f16[768,128]{1,0:T(8,128)(2,1)S(1)}, f16[768,128]{1,0:T(8,128)(2,1)S(1)}, u32[]{:S(2)}, u32[]{:S(2)}) collective-permute-start(f16[768,128]{1,0:T(8,128)(2,1)S(1)} %multiply_convert_fusion.1), channel_id=1, source_target_pairs={{1,2},{3,4},{5,6},{7,8},{9,10},{11,12},{13,14},{15,16},{17,18},{19... | collective-permute-start | bytes 589832 | tf_op jit(solution)/shard_map/ppermute | solution.py:41
  73.0 0.0 all-to-all-done.3
  73.1 0.7 broadcast_in_dim.11
  73.8 6.4 %all-to-all-start.4 = ((f16[8,32,256]{2,1,0:T(8,128)(2,1)}), f16[8,32,256]{2,1,0:T(8,128)(2,1)S(1)}, u32[]{:S(2)}, u32[]{:S(2)}) async-start(f16[8,32,256]{2,1,0:T(8,128)(2,1)} %broadcast_in_dim.11), calls=%async_computation.4 | async-start | bytes 262144 | tf_op jit(solution)/shard_map/all_to_all | solution.py:28
  80.2 2.3 %collective-permute-start.3 = (f16[768,128]{1,0:T(8,128)(2,1)S(1)}, f16[768,128]{1,0:T(8,128)(2,1)S(1)}, u32[]{:S(2)}, u32[]{:S(2)}) collective-permute-start(f16[768,128]{1,0:T(8,128)(2,1)S(1)} %multiply_convert_fusion), channel_id=1, source_target_pairs={{0,1},{1,0},{2,3},{3,2},{4,5},{5,4},{6,7},{7,6},{8,9},{9,8},{10,11... | collective-permute-start | bytes 589832 | tf_op jit(solution)/shard_map/ppermute | solution.py:36
  82.5 0.6 convert_bitcast_fusion
  83.1 0.2 all-to-all-done.4
  83.4 0.0 collective-permute-done.2
  83.4 0.2 collective-permute-done.3
  83.6 0.1 add_multiply_fusion.halo_ref
  83.6 0.8 shard_map.100
  (10 shorter events, 0.3 us)
Async XLA Ops:
  0.6 9.8 %copy-start.4 = (bf16[768,128]{1,0:T(8,128)(2,1)S(1)}, bf16[768,128]{1,0:T(8,128)(2,1)}, u32[]{:S(2)}) copy-start(bf16[768,128]{1,0:T(8,128)(2,1)} %x_ref.3) | copy-start | bytes 589828
  0.6 9.8 %copy-start = (bf16[768,2304]{1,0:T(8,128)(2,1)S(1)}, bf16[768,2304]{1,0:T(8,128)(2,1)}, u32[]{:S(2)}) copy-start(bf16[768,2304]{1,0:T(8,128)(2,1)} %adj_ref.7) | copy-start | bytes 10616836
  0.7 9.8 %copy-start.2 = (bf16[128,256]{1,0:T(8,128)(2,1)S(1)}, bf16[128,256]{1,0:T(8,128)(2,1)}, u32[]{:S(2)}) copy-start(bf16[128,256]{1,0:T(8,128)(2,1)} %wn_ref.3) | copy-start | bytes 196612
  0.7 9.8 %copy-start.1 = (bf16[128,256]{1,0:T(8,128)(2,1)S(1)}, bf16[128,256]{1,0:T(8,128)(2,1)}, u32[]{:S(2)}) copy-start(bf16[128,256]{1,0:T(8,128)(2,1)} %ws_ref.3) | copy-start | bytes 196612
  0.7 9.8 %copy-start.3 = (bf16[768,256]{1,0:T(8,128)(2,1)S(1)}, bf16[768,256]{1,0:T(8,128)(2,1)}, u32[]{:S(2)}) copy-start(bf16[768,256]{1,0:T(8,128)(2,1)} %cot_ref.1) | copy-start | bytes 1179652
  0.7 9.8 %copy-start.5 = (f32[256]{0:T(256)S(1)}, f32[256]{0:T(256)}, u32[]{:S(2)}) copy-start(f32[256]{0:T(256)} %param.10) | copy-start | bytes 3076
  0.7 10.3 %collective-permute-start.1 = (bf16[768,128]{1,0:T(8,128)(2,1)}, bf16[768,128]{1,0:T(8,128)(2,1)S(1)}, u32[]{:S(2)}, u32[]{:S(2)}) collective-permute-start(bf16[768,128]{1,0:T(8,128)(2,1)} %x_ref.3), channel_id=1, source_target_pairs={{1,2},{3,4},{5,6},{7,8},{9,10},{11,12},{13,14},{15,16},{17,18},{19... | collective-permute-start | bytes 589832 | tf_op jit(solution)/shard_map/ppermute | solution.py:41
  5.5 6.2 %collective-permute-start = (bf16[768,128]{1,0:T(8,128)(2,1)}, bf16[768,128]{1,0:T(8,128)(2,1)S(1)}, u32[]{:S(2)}, u32[]{:S(2)}) collective-permute-start(bf16[768,128]{1,0:T(8,128)(2,1)} %x_ref.3), channel_id=1, source_target_pairs={{0,1},{1,0},{2,3},{3,2},{4,5},{5,4},{6,7},{7,6},{8,9},{9,8},{10,11... | collective-permute-start | bytes 589832 | tf_op jit(solution)/shard_map/ppermute | solution.py:36
  60.9 12.1 %all-to-all-start.3 = ((f16[8,32,256]{2,1,0:T(8,128)(2,1)}), f16[8,32,256]{2,1,0:T(8,128)(2,1)S(1)}, u32[]{:S(2)}, u32[]{:S(2)}) async-start(f16[8,32,256]{2,1,0:T(8,128)(2,1)} %broadcast_in_dim.10), calls=%async_computation.3 | async-start | bytes 262144 | tf_op jit(solution)/shard_map/all_to_all | solution.py:32
  69.8 13.6 %collective-permute-start.2 = (f16[768,128]{1,0:T(8,128)(2,1)S(1)}, f16[768,128]{1,0:T(8,128)(2,1)S(1)}, u32[]{:S(2)}, u32[]{:S(2)}) collective-permute-start(f16[768,128]{1,0:T(8,128)(2,1)S(1)} %multiply_convert_fusion.1), channel_id=1, source_target_pairs={{1,2},{3,4},{5,6},{7,8},{9,10},{11,12},{13,14},{15,16},{17,18},{19... | collective-permute-start | bytes 589832 | tf_op jit(solution)/shard_map/ppermute | solution.py:41
  73.8 9.6 %all-to-all-start.4 = ((f16[8,32,256]{2,1,0:T(8,128)(2,1)}), f16[8,32,256]{2,1,0:T(8,128)(2,1)S(1)}, u32[]{:S(2)}, u32[]{:S(2)}) async-start(f16[8,32,256]{2,1,0:T(8,128)(2,1)} %broadcast_in_dim.11), calls=%async_computation.4 | async-start | bytes 262144 | tf_op jit(solution)/shard_map/all_to_all | solution.py:28
  80.2 3.4 %collective-permute-start.3 = (f16[768,128]{1,0:T(8,128)(2,1)S(1)}, f16[768,128]{1,0:T(8,128)(2,1)S(1)}, u32[]{:S(2)}, u32[]{:S(2)}) collective-permute-start(f16[768,128]{1,0:T(8,128)(2,1)S(1)} %multiply_convert_fusion), channel_id=1, source_target_pairs={{0,1},{1,0},{2,3},{3,2},{4,5},{5,4},{6,7},{7,6},{8,9},{9,8},{10,11... | collective-permute-start | bytes 589832 | tf_op jit(solution)/shard_map/ppermute | solution.py:36

commit v7 on v6

--- a/solution.py
+++ b/solution.py
@@ -104,14 +104,14 @@
     def back(slab):
         return mm(scaled, slabs(adj_ref, slab, 1))
 
-    far_ref[...] = back(2 * core).T
-    near_ref[...] = back(2 - 2 * core).T
-    mid_ref[...] = (back(1) + mm(ws_ref[...], dpre)).T
+    far_ref[...] = back(2 * core)
+    near_ref[...] = back(2 - 2 * core)
+    mid_ref[...] = back(1) + mm(ws_ref[...], dpre)
 
 
 def finish_kernel(grad_ref, mid_ref, halo_ref, total_ref, self_ref, neigh_ref):
     feats = self_ref.shape[0]
-    total_ref[...] = (mid_ref[...] + halo_ref[...]).astype(BF16)
+    total_ref[...] = (mid_ref[...] + halo_ref[...]).T.astype(BF16)
     self_ref[...] = grad_ref[:feats]
     neigh_ref[...] = grad_ref[feats:]
 
@@ -180,7 +180,7 @@
         back_kernel,
         in_specs=[VMEM] * 5,
         out_specs=[VMEM] * 3,
-        out_shape=[shape((rows, feats), F32)] * 3,
+        out_shape=[shape((feats, rows), F32)] * 3,
         compiler_params=PARAMS,
         cost_estimate=pl.CostEstimate(flops=6 * rows * rows * feats, bytes_accessed=6 * rows * rows, transcendentals=0),
     )(adjacency, deg, w_self, w_neigh, dpre)

time: 85 us -> 84.9 us (level)
  no operation moved by 1% of the time
where the time goes in v7:
time: 84.9 us; the launch traced here: 84.3 us
  blocking collectives  46.2 us (54%)
  starting transfers between devices  30.5 us (36%)
  Pallas kernels  3.92 us (5%)
  local copies, waits for them, and re-layouts  1.36 us (2%)
  other arithmetic  0.95 us (1%)
  between operations  0.89 us (1%)
    all_to_all x2, blocking collectives, exchange_down(): lax.all_to_all(blocks, axes, 0, 0, tiled=True, axis_index_groups=[list(ra...  23.3 us
    all_to_all x1, blocking collectives, exchange(): return lax.all_to_all(blocks, axes, 0, 0, tiled=True)  22.9 us
    all_to_all x1, starting transfers between devices, exchange_rows(): lax.all_to_all(blocks, 'y', 0, 0, tiled=True, axis_index_groups=[[4, 5, 3...  8.85 us
    ppermute x2, starting transfers between devices, swap_chips(): return lax.ppermute(block, VERT, pairs + [(j, i) for i, j in pairs])  7.96 us
    ppermute x2, starting transfers between devices, swap_cores(): return lax.ppermute(block, 'c', [(0, 1), (1, 0)])  7.29 us
    all_to_all x1, starting transfers between devices, exchange_down(): lax.all_to_all(blocks, axes, 0, 0, tiled=True, axis_index_groups=[list(ra...  6.37 us
  transfers between devices with their start and end apart: 6, of which 3 were waited for; matrix products, arithmetic and copies ran while one was open for 2% of the time, Pallas kernels for 1%

profile of v7, /device:TPU:1, one launch (start us, length us, event | category | flops | bytes accessed | tf_op | source)
XLA Modules:
  0.0 84.3 jit_solution(5605818652938315648)
XLA Ops:
  0.6 0.0 copy-start.4
  0.6 0.0 copy-start
  0.7 0.0 copy-start.2
  0.7 0.0 copy-start.1
  0.7 0.0 copy-start.3
  0.7 0.0 copy-start.5
  0.7 4.8 %collective-permute-start.1 = (bf16[768,128]{1,0:T(8,128)(2,1)}, bf16[768,128]{1,0:T(8,128)(2,1)S(1)}, u32[]{:S(2)}, u32[]{:S(2)}) collective-permute-start(bf16[768,128]{1,0:T(8,128)(2,1)} %x_ref.3), channel_id=1, source_target_pairs={{1,2},{3,4},{5,6},{7,8},{9,10},{11,12},{13,14},{15,16},{17,18},{19... | collective-permute-start | bytes 589832 | tf_op jit(solution)/shard_map/ppermute | solution.py:41
  5.5 5.0 %collective-permute-start = (bf16[768,128]{1,0:T(8,128)(2,1)}, bf16[768,128]{1,0:T(8,128)(2,1)S(1)}, u32[]{:S(2)}, u32[]{:S(2)}) collective-permute-start(bf16[768,128]{1,0:T(8,128)(2,1)} %x_ref.3), channel_id=1, source_target_pairs={{0,1},{1,0},{2,3},{3,2},{4,5},{5,4},{6,7},{7,6},{8,9},{9,8},{10,11... | collective-permute-start | bytes 589832 | tf_op jit(solution)/shard_map/ppermute | solution.py:36
  10.5 0.0 copy-done.4
  10.5 0.0 copy-done
  10.5 0.0 copy-done.2
  10.5 0.0 copy-done.1
  10.5 0.0 copy-done.3
  10.5 0.0 copy-done.5
  10.5 0.5 shard_map.94
  11.0 0.0 collective-permute-done.1.far_ref
  11.0 0.5 shard_map.95.sum_ref
  11.5 0.2 collective-permute-done.near_ref
  11.7 0.8 shard_map.96
  12.6 22.9 %all_to_all.25 = f16[8,32,768]{2,1,0:T(8,128)(2,1)S(1)} all-to-all(f16[8,32,768]{2,1,0:T(8,128)(2,1)S(1)} %bitcast.11), channel_id=1, replica_groups=mesh['z'=8,'y'=8,'x'=4,'c'=2] {'z'}, dimensions={0} | all-to-all | bytes 786432 | tf_op jit(solution)/shard_map/all_to_all | solution.py:24
  35.4 0.1 convert_reduce_fusion.pre_ref
  35.5 0.1 shard_map.97
  35.6 13.2 %all_to_all.26 = bf16[8,32,768]{2,1,0:T(8,128)(2,1)S(1)} all-to-all(bf16[8,32,768]{2,1,0:T(8,128)(2,1)S(1)} %get-tuple-element.40), channel_id=1, replica_groups={{448,384,320,256,192,128,64,0},{449,385,321,257,193,129,65,1},{450,386,..., dimensions={0} | all-to-all | bytes 786432 | tf_op jit(solution)/shard_map/all_to_all | solution.py:28
  48.8 0.3 shard_map.98
  49.1 0.9 %shard_map.99 = (f32[128,768]{1,0:T(8,128)S(1)}, f32[128,768]{1,0:T(8,128)S(1)}, f32[128,768]{1,0:T(8,128)S(1)}) custom-call(bf16[768,2304]{1,0:T(8,128)(2,1)S(1)} %copy-done, f32[8,768]{1,0:T(8,128)S(1)} %get-tuple-element.43.deg_ref, bf16[128,256]{1,0:T(8,128)(2,1)S(1)} %copy-done.1, bf16[128,256]{1,0:T(8,128)(2,1)S(1)} %copy-done.2, ...), custom_call_target="tpu_custom_call" | custom-call | flops 452984832 | bytes 3538944 | tf_op jit(solution)/shard_map/pallas_call | solution.py:179
  50.0 10.1 %all_to_all.27 = f16[8,32,256]{2,1,0:T(8,128)(2,1)S(1)} all-to-all(f16[8,32,256]{2,1,0:T(8,128)(2,1)S(1)} %bitcast.12), channel_id=1, replica_groups={{7,6,5,4,3,2,1,0},{15,14,13,12,11,10,9,8},{23,22,21,20,19,18,17,16},{31..., dimensions={0} | all-to-all | bytes 262144 | tf_op jit(solution)/shard_map/all_to_all | solution.py:28
  60.2 0.7 broadcast_in_dim.10
  60.9 8.9 %all-to-all-start.3 = ((f16[8,32,256]{2,1,0:T(8,128)(2,1)}), f16[8,32,256]{2,1,0:T(8,128)(2,1)S(1)}, u32[]{:S(2)}, u32[]{:S(2)}) async-start(f16[8,32,256]{2,1,0:T(8,128)(2,1)} %broadcast_in_dim.10), calls=%async_computation.3 | async-start | bytes 262144 | tf_op jit(solution)/shard_map/all_to_all | solution.py:32
  69.7 3.2 %collective-permute-start.2 = (f16[128,768]{1,0:T(8,128)(2,1)S(1)}, f16[128,768]{1,0:T(8,128)(2,1)S(1)}, u32[]{:S(2)}, u32[]{:S(2)}) collective-permute-start(f16[128,768]{1,0:T(8,128)(2,1)S(1)} %multiply_convert_fusion.1), channel_id=1, source_target_pairs={{1,2},{3,4},{5,6},{7,8},{9,10},{11,12},{13,14},{15,16},{17,18},{19... | collective-permute-start | bytes 589832 | tf_op jit(solution)/shard_map/ppermute | solution.py:41
  72.9 0.0 all-to-all-done.3
  73.0 0.7 broadcast_in_dim.11
  73.7 6.4 %all-to-all-start.4 = ((f16[8,32,256]{2,1,0:T(8,128)(2,1)}), f16[8,32,256]{2,1,0:T(8,128)(2,1)S(1)}, u32[]{:S(2)}, u32[]{:S(2)}) async-start(f16[8,32,256]{2,1,0:T(8,128)(2,1)} %broadcast_in_dim.11), calls=%async_computation.4 | async-start | bytes 262144 | tf_op jit(solution)/shard_map/all_to_all | solution.py:28
  80.1 2.3 %collective-permute-start.3 = (f16[128,768]{1,0:T(8,128)(2,1)S(1)}, f16[128,768]{1,0:T(8,128)(2,1)S(1)}, u32[]{:S(2)}, u32[]{:S(2)}) collective-permute-start(f16[128,768]{1,0:T(8,128)(2,1)S(1)} %multiply_convert_fusion), channel_id=1, source_target_pairs={{0,1},{1,0},{2,3},{3,2},{4,5},{5,4},{6,7},{7,6},{8,9},{9,8},{10,11... | collective-permute-start | bytes 589832 | tf_op jit(solution)/shard_map/ppermute | solution.py:36
  82.4 0.6 convert_bitcast_fusion
  83.0 0.2 all-to-all-done.4
  83.3 0.0 collective-permute-done.2
  83.3 0.1 collective-permute-done.3
  83.5 0.1 add_multiply_fusion.halo_ref
  83.5 0.8 shard_map.100
  (10 shorter events, 0.2 us)
Async XLA Ops:
  0.6 9.8 %copy-start.4 = (bf16[768,128]{1,0:T(8,128)(2,1)S(1)}, bf16[768,128]{1,0:T(8,128)(2,1)}, u32[]{:S(2)}) copy-start(bf16[768,128]{1,0:T(8,128)(2,1)} %x_ref.3) | copy-start | bytes 589828
  0.6 9.8 %copy-start = (bf16[768,2304]{1,0:T(8,128)(2,1)S(1)}, bf16[768,2304]{1,0:T(8,128)(2,1)}, u32[]{:S(2)}) copy-start(bf16[768,2304]{1,0:T(8,128)(2,1)} %adj_ref.7) | copy-start | bytes 10616836
  0.7 9.8 %copy-start.2 = (bf16[128,256]{1,0:T(8,128)(2,1)S(1)}, bf16[128,256]{1,0:T(8,128)(2,1)}, u32[]{:S(2)}) copy-start(bf16[128,256]{1,0:T(8,128)(2,1)} %wn_ref.3) | copy-start | bytes 196612
  0.7 9.8 %copy-start.1 = (bf16[128,256]{1,0:T(8,128)(2,1)S(1)}, bf16[128,256]{1,0:T(8,128)(2,1)}, u32[]{:S(2)}) copy-start(bf16[128,256]{1,0:T(8,128)(2,1)} %ws_ref.3) | copy-start | bytes 196612
  0.7 9.8 %copy-start.3 = (bf16[768,256]{1,0:T(8,128)(2,1)S(1)}, bf16[768,256]{1,0:T(8,128)(2,1)}, u32[]{:S(2)}) copy-start(bf16[768,256]{1,0:T(8,128)(2,1)} %cot_ref.1) | copy-start | bytes 1179652
  0.7 9.8 %copy-start.5 = (f32[256]{0:T(256)S(1)}, f32[256]{0:T(256)}, u32[]{:S(2)}) copy-start(f32[256]{0:T(256)} %param.10) | copy-start | bytes 3076
  0.7 10.3 %collective-permute-start.1 = (bf16[768,128]{1,0:T(8,128)(2,1)}, bf16[768,128]{1,0:T(8,128)(2,1)S(1)}, u32[]{:S(2)}, u32[]{:S(2)}) collective-permute-start(bf16[768,128]{1,0:T(8,128)(2,1)} %x_ref.3), channel_id=1, source_target_pairs={{1,2},{3,4},{5,6},{7,8},{9,10},{11,12},{13,14},{15,16},{17,18},{19... | collective-permute-start | bytes 589832 | tf_op jit(solution)/shard_map/ppermute | solution.py:41
  5.5 6.2 %collective-permute-start = (bf16[768,128]{1,0:T(8,128)(2,1)}, bf16[768,128]{1,0:T(8,128)(2,1)S(1)}, u32[]{:S(2)}, u32[]{:S(2)}) collective-permute-start(bf16[768,128]{1,0:T(8,128)(2,1)} %x_ref.3), channel_id=1, source_target_pairs={{0,1},{1,0},{2,3},{3,2},{4,5},{5,4},{6,7},{7,6},{8,9},{9,8},{10,11... | collective-permute-start | bytes 589832 | tf_op jit(solution)/shard_map/ppermute | solution.py:36
  60.9 12.1 %all-to-all-start.3 = ((f16[8,32,256]{2,1,0:T(8,128)(2,1)}), f16[8,32,256]{2,1,0:T(8,128)(2,1)S(1)}, u32[]{:S(2)}, u32[]{:S(2)}) async-start(f16[8,32,256]{2,1,0:T(8,128)(2,1)} %broadcast_in_dim.10), calls=%async_computation.3 | async-start | bytes 262144 | tf_op jit(solution)/shard_map/all_to_all | solution.py:32
  69.7 13.6 %collective-permute-start.2 = (f16[128,768]{1,0:T(8,128)(2,1)S(1)}, f16[128,768]{1,0:T(8,128)(2,1)S(1)}, u32[]{:S(2)}, u32[]{:S(2)}) collective-permute-start(f16[128,768]{1,0:T(8,128)(2,1)S(1)} %multiply_convert_fusion.1), channel_id=1, source_target_pairs={{1,2},{3,4},{5,6},{7,8},{9,10},{11,12},{13,14},{15,16},{17,18},{19... | collective-permute-start | bytes 589832 | tf_op jit(solution)/shard_map/ppermute | solution.py:41
  73.7 9.6 %all-to-all-start.4 = ((f16[8,32,256]{2,1,0:T(8,128)(2,1)}), f16[8,32,256]{2,1,0:T(8,128)(2,1)S(1)}, u32[]{:S(2)}, u32[]{:S(2)}) async-start(f16[8,32,256]{2,1,0:T(8,128)(2,1)} %broadcast_in_dim.11), calls=%async_computation.4 | async-start | bytes 262144 | tf_op jit(solution)/shard_map/all_to_all | solution.py:28
  80.1 3.4 %collective-permute-start.3 = (f16[128,768]{1,0:T(8,128)(2,1)S(1)}, f16[128,768]{1,0:T(8,128)(2,1)S(1)}, u32[]{:S(2)}, u32[]{:S(2)}) collective-permute-start(f16[128,768]{1,0:T(8,128)(2,1)S(1)} %multiply_convert_fusion), channel_id=1, source_target_pairs={{0,1},{1,0},{2,3},{3,2},{4,5},{5,4},{6,7},{7,6},{8,9},{9,8},{10,11... | collective-permute-start | bytes 589832 | tf_op jit(solution)/shard_map/ppermute | solution.py:36
